TPU v7x, 256 devices: a whole 4x4x8 slice. The times are simulated.
256 devices in a mesh: grp: 8 (over z), seq: 32 (over x, y, core).
Axes of the slice: x: 4, y: 4, z: 8, core: 2. Of those that a mesh axis runs over, the one named last changes fastest.
Arguments:
- frames: bfloat16 [8, 16384, 1024], P('grp', 'seq'), may hold values from -6 to 6
- begins: int32 [8, 16384], P('grp', 'seq'), may hold values from 0 to 1, as said below
- owner: int32 [8, 2048, 1], P('grp', 'seq'), may hold values from 0 to 31; in each aligned block of 64 rows (0 to 63, 64 to 127, ..., all dimensions but the last counted through in order) at most 4 rows name the same one
- conv_kernel: float32 [9, 1024], replicated, may hold values from -2 to 2
- norm_gain: float32 [1024], replicated, may hold values from 0.25 to 1.75
- w_qkv: bfloat16 [1024, 3072], replicated, may hold values from -0.1875 to 0.1875
- w_out: bfloat16 [1024, 1024], replicated, may hold values from -1 to 1
- cotangent: bfloat16 [8, 4096, 1024], P('grp', 'seq'), may hold values from -6 to 6
Outputs:
- audio_rows: bfloat16 [8, 4096, 1024], P('grp', 'seq')
- out_grad: bfloat16 [1024, 1024], replicated
Inputs may be any that keep to these rules, and one draw needn't show every extreme that they name: `begins`: the first frame of every group is 1; utterances run 16 frames or more and fewer than 1536, the last one cut by the group's end. At most 4 pooled rows of one device go to one owner.
All inputs are finite; a program needn't handle non-finite values.
Results may differ from a plain program's by a relative error of at most 0.017.
The roundings to bfloat16 on the way count: a program that leaves them out, or rounds other values in their place, can miss the bound.
Values may be sent and summed in bfloat16 or wider, within the bound.
A program may use at most 128 MiB of HBM per device.

v0:
```python
import jax
import jax.numpy as jnp
from jax import lax
from jax.sharding import PartitionSpec as P

HEADS = 8
BLOCK_LEN = 32
LEFT_BLOCKS = 2
SUB = 8


def entering(part, axis, combine, identity, reverse):
    count = lax.axis_size(axis)
    place = lax.axis_index(axis)
    ahead = count - 1 - place if reverse else place
    gathered = lax.all_gather(part, axis)
    state = jnp.zeros_like(part) + jnp.asarray(identity, part.dtype)

    def one(hop, state):
        source = count - 1 - hop if reverse else hop
        return combine(state, lax.dynamic_index_in_dim(gathered, source, 0, False))

    return lax.fori_loop(0, ahead, one, state)


def with_halo(block, sides, width):
    for axis, dim in sides:
        count = lax.axis_size(axis)
        forward = [(i, i + 1) for i in range(count - 1)]
        backward = [(target, source) for source, target in forward]
        low = lax.ppermute(
            lax.slice_in_dim(block, block.shape[dim] - width, None, axis=dim), axis, forward
        )
        high = lax.ppermute(lax.slice_in_dim(block, 0, width, axis=dim), axis, backward)
        block = jnp.concatenate([low, block, high], axis=dim)
    return block


def shifted(array, axis, by):
    devices = lax.axis_size(axis)
    pairs = [(i, i + by) for i in range(devices) if 0 <= i + by < devices]
    return lax.ppermute(array, axis, pairs)


def layer_norm(hidden, norm_gain):
    values = hidden.astype(jnp.float32)
    centred = values - jnp.mean(values, axis=-1, keepdims=True)
    spread = jnp.mean(centred * centred, axis=-1, keepdims=True)
    return (centred * lax.rsqrt(spread + 1e-05) * norm_gain).astype(jnp.bfloat16)


def shards(frames, begins, owner, conv_kernel, norm_gain, w_qkv, w_out, cotangent):
    seq_count = lax.axis_size("seq")
    grp_count = lax.axis_size("grp")
    frame_count = frames.shape[1]
    width = frames.shape[2]
    group_len = frame_count * seq_count
    offset = lax.axis_index("seq") * frame_count
    frame_idx = offset + jnp.arange(frame_count, dtype=jnp.int32)
    begin_mask = begins[0] == 1
    marked = jnp.where(begin_mask, frame_idx, -1)
    last_mark = jnp.max(marked).reshape(1)
    earlier = entering(last_mark, "seq", jnp.maximum, jnp.full((1,), -1, jnp.int32), False)
    start_idx = jnp.maximum(lax.cummax(marked, axis=0), earlier[0])
    ahead_idx = jnp.where(begin_mask, frame_idx, group_len)
    first_mark = jnp.min(ahead_idx).reshape(1)
    later_mark = entering(
        first_mark, "seq", jnp.minimum, jnp.full((1,), group_len, jnp.int32), True
    )
    next_local = jnp.concatenate(
        [lax.cummin(ahead_idx, axis=0, reverse=True)[1:], jnp.full((1,), group_len, jnp.int32)]
    )
    stop_idx = jnp.minimum(next_local, later_mark[0])
    reach = conv_kernel.shape[0] // 2
    padded = with_halo(frames, (("seq", 1),), reach)[0]
    conv_sum = jnp.zeros((frame_count, width), jnp.float32)
    for tap in range(conv_kernel.shape[0]):
        source_idx = frame_idx + tap - reach
        inside = (source_idx >= start_idx) & (source_idx < stop_idx)
        term = padded[tap : tap + frame_count].astype(jnp.float32) * conv_kernel[tap]
        conv_sum = conv_sum + jnp.where(inside[:, None], term, jnp.float32(0.0))
    hidden = (frames[0].astype(jnp.float32) + conv_sum).astype(jnp.bfloat16)
    qkv = jnp.dot(layer_norm(hidden, norm_gain), w_qkv, preferred_element_type=jnp.float32).astype(
        jnp.bfloat16
    )
    queries = qkv[:, :width]
    keyval = qkv[:, width:]
    left_reach = (LEFT_BLOCKS + 1) * BLOCK_LEN
    right_reach = BLOCK_LEN
    left_kv = shifted(keyval[frame_count - left_reach :], "seq", 1)
    right_kv = shifted(keyval[:right_reach], "seq", -1)
    keys_all = jnp.concatenate([left_kv, keyval, right_kv], axis=0)
    query_block = min(512, frame_count)
    span = query_block + left_reach + right_reach
    head_dim = width // HEADS
    query_rows = queries.reshape(query_block, HEADS, head_dim)
    key_heads = keys_all[:, :width].reshape(span, HEADS, head_dim)
    value_heads = keys_all[:, width:].reshape(span, HEADS, head_dim)
    key_idx = offset + 0 - left_reach + jnp.arange(span, dtype=jnp.int32)
    query_pos = (frame_idx - start_idx) // BLOCK_LEN
    key_pos = (key_idx[None, :] - start_idx[:, None]) // BLOCK_LEN
    allowed = (key_idx[None, :] >= start_idx[:, None]) & (key_idx[None, :] < stop_idx[:, None])
    allowed = (
        allowed & (key_pos >= query_pos[:, None] - LEFT_BLOCKS) & (key_pos <= query_pos[:, None])
    )
    scores = jnp.einsum("qhd,khd->hqk", query_rows, key_heads, preferred_element_type=jnp.float32)
    scores = scores / jnp.sqrt(jnp.float32(head_dim))
    scores = jnp.where(allowed[None], scores, jnp.float32(-1e30))
    top = jnp.max(scores, axis=-1, keepdims=True)
    expo = jnp.exp(scores - top)
    weights = (expo / jnp.sum(expo, axis=-1, keepdims=True)).astype(jnp.bfloat16)
    mixed = jnp.einsum("hqk,khd->qhd", weights, value_heads, preferred_element_type=jnp.float32)
    pieces = mixed.reshape(query_block, width).astype(jnp.bfloat16)
    outputs = hidden.astype(jnp.float32) + jnp.dot(
        pieces, w_out, preferred_element_type=jnp.float32
    )
    row_count = frame_count // SUB
    pooled = jnp.mean(outputs.reshape(row_count, SUB, width), axis=1).astype(jnp.bfloat16)
    slot_cap = cotangent.shape[1] // seq_count
    destination = owner[0, :, 0]
    onehot = (destination[:, None] == jnp.arange(seq_count, dtype=jnp.int32)[None, :]).astype(
        jnp.int32
    )
    before = jnp.cumsum(onehot, axis=0) - onehot
    rank_index = jnp.sum(onehot * before, axis=1)
    slot_index = destination * slot_cap + rank_index
    placement = (
        slot_index[None, :] == jnp.arange(seq_count * slot_cap, dtype=jnp.int32)[:, None]
    ).astype(jnp.bfloat16)
    outgoing = jnp.dot(placement, pooled, preferred_element_type=jnp.float32).astype(jnp.bfloat16)
    incoming = lax.all_to_all(
        outgoing.reshape(seq_count, slot_cap, width), "seq", split_axis=0, concat_axis=0, tiled=True
    )
    audio_rows = incoming.reshape(1, seq_count * slot_cap, width)
    returned = lax.all_to_all(
        cotangent[0].reshape(seq_count, slot_cap, width),
        "seq",
        split_axis=0,
        concat_axis=0,
        tiled=True,
    )
    row_grads = lax.dot_general(
        placement,
        returned.reshape(seq_count * slot_cap, width),
        (((0,), (0,)), ((), ())),
        preferred_element_type=jnp.float32,
    )
    grad_scale = 1.0 / jnp.sqrt(jnp.float32(grp_count * seq_count * row_count))
    frame_grads = jnp.repeat(row_grads / SUB, SUB, axis=0).astype(jnp.bfloat16)
    local_grad = lax.dot_general(
        pieces, frame_grads, (((0,), (0,)), ((), ())), preferred_element_type=jnp.float32
    )
    local_grad = local_grad * grad_scale
    grad_total = lax.psum(local_grad, ("grp", "seq"))
    out_grad = grad_total.astype(jnp.bfloat16)
    return (audio_rows, out_grad)


def solution(mesh):
    return jax.shard_map(
        shards,
        mesh=mesh,
        in_specs=(
            P("grp", "seq", None),
            P("grp", "seq"),
            P("grp", "seq", None),
            P(),
            P(),
            P(),
            P(),
            P("grp", "seq", None),
        ),
        out_specs=(P("grp", "seq", None), P()),
        check_vma=False,
    )
```

profile of v0, /device:TPU:1, one launch (start us, length us, event | category | flops | bytes accessed | tf_op | source)
XLA Modules:
  0.0 291.6 jit_solution(8263604999376667804)
XLA Ops:
  0.7 1.5 fusion.104
  2.2 5.1 %collective-permute-start.1 = (bf16[1,4,1024]{2,1,0:T(4,128)(2,1)}, bf16[1,4,1024]{2,1,0:T(4,128)(2,1)}, u32[]{:S(2)}, u32[]{:S(2)}) collective-permute-start(bf16[1,4,1024]{2,1,0:T(4,128)(2,1)} %get-tuple-element.113), channel_id=1, source_target_pairs={{1,0},{2,1},{3,2},{4,3},{5,4},{6,5},{7,6},{8,7},{9,8},{10,9},{11,1... | collective-permute-start | bytes 24584 | tf_op jit(solution)/shard_map/ppermute | solution.py:34
  7.3 1.9 collective-permute-start
  9.2 1.8 reshape_squeeze.3
  11.0 8.5 %all-to-all-start.1 = ((bf16[32,4,1024]{2,1,0:T(4,128)(2,1)}), bf16[32,4,1024]{2,1,0:T(4,128)(2,1)S(1)}, u32[]{:S(2)}, u32[]{:S(2)}) async-start(bf16[32,4,1024]{2,1,0:T(4,128)(2,1)} %reshape_squeeze.3), calls=%async_computation.1 | async-start | bytes 524288 | tf_op jit(solution)/shard_map/all_to_all | solution.py:135
  24.9 13.3 %all-reduce.2 = (s32[32]{0:T(128)S(1)}, s32[32]{0:T(128)S(1)}) all-reduce(s32[32]{0:T(128)S(1)} %dynamic-update-slice, s32[32]{0:T(128)S(1)} %dynamic-update-slice.1), channel_id=1, replica_groups=mesh['grp'=8,'seq'=32] {'seq'}, use_global_device_ids=true, to_apply=%add | all-reduce | flops 64 | bytes 512
  39.9 35.0 %while.23 = (s32[]{:T(128)}, s32[1]{0:T(128)}, s32[]{:T(128)}, s32[32,1]{0,1:T(1,128)S(1)}, s32[]{:T(128)}, /*index=5*/s32[]{:T(128)}, s32[]{:T(128)}, s32[]{:T(128)}) while((s32[]{:T(128)}, s32[1]{0:T(128)}, s32[]{:T(128)}, s32[32,1]{0,1:T(1,128)S(1)}, s32[]{:T(128)}, /*index=5*/s32[]{:T(128)}, s32[]{:T(128)}, s32[]{:T(128)}) %tuple.73), condition=%wide.region_11.12_spmd, body=%wide.region_10.11_spmd.sunk | while | flops 7 | bytes 163 | solution.py:23
  74.9 2.3 reduce-window.24
  79.7 2.0 compare_and_fusion
  83.3 8.4 %convert_reduce_fusion = (f32[512]{0:T(512)S(1)}, bf16[512,1024]{1,0:T(8,128)(2,1)S(1)}) fusion(f32[1024]{0:T(1024)S(1)} %bitcast.123, bf16[1,516,1024]{2,1,0:T(8,128)(2,1)S(1)} %constant_dynamic-update-slice_fusion, pred[512]{0:T(512)(128)(4,1)} %get-tuple-element.124, f32[1024]{0:T(1024)S(1)} %bitcast.124, pred[512]{0:T(512)(128)(4,1)} %get-tuple-element.125, ...), kind=kLoop, calls=%fused_computation.14 | loop fusion | flops 28835328 | bytes 6343168 | tf_op jit(solution)/shard_map/reduce_sum | solution.py:47
  92.2 4.0 %convolution_convert_fusion = bf16[512,3072]{1,0:T(8,128)(2,1)S(1)} fusion(bf16[1024,3072]{1,0:T(8,128)(2,1)S(1)} %copy-done.12, bf16[512,1024]{1,0:T(8,128)(2,1)S(1)} %get-tuple-element.107, f32[1024]{0:T(1024)S(1)} %copy-done.13, f32[512]{0:T(512)S(1)} %add_rsqrt_fusion, f32[512]{0:T(512)S(1)} %broadcast_multiply_fusion), kind=kOutput, calls=%fused_computation.11 | convolution fusion | flops 3225419776 | bytes 10493952 | tf_op jit(solution)/shard_map/dot_general | solution.py:83
  96.3 5.6 %collective-permute-start.2 = (bf16[96,2048]{1,0:T(8,128)(2,1)S(1)}, bf16[96,2048]{1,0:T(8,128)(2,1)S(1)}, u32[]{:S(2)}, u32[]{:S(2)}) collective-permute-start(bf16[96,2048]{1,0:T(8,128)(2,1)S(1)} %slice.152), channel_id=1, source_target_pairs={{0,1},{1,2},{2,3},{3,4},{4,5},{5,6},{6,7},{7,8},{8,9},{9,10},{10,1... | collective-permute-start | bytes 1179656 | tf_op jit(solution)/shard_map/ppermute | solution.py:42
  102.5 1.5 slice.153
  104.1 2.1 collective-permute-start.3
  107.1 3.4 %collective-permute-done.3 = bf16[32,2048]{1,0:T(8,128)(2,1)S(1)} collective-permute-done((bf16[32,2048]{1,0:T(8,128)(2,1)}, bf16[32,2048]{1,0:T(8,128)(2,1)S(1)}, u32[]{:S(2)}, u32[]{:S(2)}) %collective-permute-start.3) | collective-permute-done | bytes 131104 | tf_op jit(solution)/shard_map/ppermute | solution.py:42
  110.5 1.9 pad_maximum_fusion
  113.9 2.4 copy.16
  116.3 6.8 %fusion.36 = f32[8,512,640]{2,1,0:T(8,128)} fusion(bf16[80,8,8,128]{3,2,1,0:T(8,128)(2,1)S(1)} %get-tuple-element.110, bf16[512,3072]{1,0:T(8,128)(2,1)} %copy-done.1), kind=kOutput, calls=%fused_computation.67 | convolution fusion | flops 671088640 | bytes 12845056 | tf_op jit(solution)/shard_map/qhd,khd->hqk/dot_general | solution.py:106
  123.1 15.3 %fusion.106 = (f32[8,512]{1,0:T(8,128)S(1)}, f32[8,512,640]{2,1,0:T(8,128)}) fusion(f32[8,512,640]{2,1,0:T(8,128)} %fusion.36, pred[512,640]{1,0:T(8,128)(4,1)S(1)} %copy-done.5), kind=kOutput, calls=%fused_computation.172 | output fusion | flops 15729279 | bytes 21315584 | tf_op jit(solution)/shard_map/sub | solution.py:110
  138.4 6.0 %fusion.31 = bf16[8,128,512]{2,1,0:T(8,128)(2,1)S(1)} fusion(bf16[640,8,128]{0,2,1:T(8,128)(2,1)S(1)} %bitcast.114, f32[8,512,640]{2,1,0:T(8,128)} %get-tuple-element.134, f32[8,512]{1,0:T(8,128)S(1)} %get-tuple-element.133), kind=kOutput, calls=%fused_computation.62 | convolution fusion | flops 676855808 | bytes 12861440 | tf_op jit(solution)/shard_map/hqk,khd->qhd/dot_general | solution.py:112
  144.5 1.6 fusion.19
  147.1 7.4 %all-to-all-start = ((bf16[32,4,1024]{2,1,0:T(4,128)(2,1)}), bf16[32,4,1024]{2,1,0:T(4,128)(2,1)S(1)}, u32[]{:S(2)}, u32[]{:S(2)}) async-start(bf16[32,4,1024]{2,1,0:T(4,128)(2,1)} %reshape.505), calls=%async_computation | async-start | bytes 524288 | tf_op jit(solution)/shard_map/all_to_all | solution.py:131
  154.6 3.2 %convolution_multiply_fusion = f32[1024,1024]{1,0:T(8,128)} fusion(bf16[512,1024]{0,1:T(8,128)(2,1)S(1)} %bitcast.128, bf16[64,1024]{1,0:T(8,128)(2,1)S(1)} %copy-done.6), kind=kOutput, calls=%fused_computation.24 | convolution fusion | flops 1074790400 | bytes 5373952 | tf_op jit(solution)/shard_map/dot_general | solution.py:150
  157.8 133.0 %all-reduce.4 = bf16[1024,1024]{1,0:T(8,128)(2,1)} all-reduce(f32[1024,1024]{1,0:T(8,128)} %convolution_multiply_fusion), channel_id=1, replica_groups=mesh['grp'=8,'seq'=32] {'grp','seq'}, use_global_device_ids=true, to_apply=%region_17.18 | all-reduce | flops 1048576 | bytes 6291456 | tf_op jit(solution)/shard_map/psum | solution.py:154
  (105 shorter events, 34.3 us)
Async XLA Ops:
  0.6 143.8 %copy-start = (bf16[1024,1024]{1,0:T(8,128)(2,1)S(1)}, bf16[1024,1024]{1,0:T(8,128)(2,1)}, u32[]{:S(2)}) copy-start(bf16[1024,1024]{1,0:T(8,128)(2,1)} %param.18) | copy-start | bytes 6291460
  0.6 20.9 %copy-start.14 = (u32[256]{0:T(256)S(1)}, u32[256]{0:T(256)}, u32[]{:S(2)}) copy-start(u32[256]{0:T(256)} %constant.171) | copy-start | bytes 3076
  0.7 20.1 %copy-start.11 = (s32[1,512]{1,0:T(1,128)S(1)}, s32[1,512]{1,0:T(1,128)}, u32[]{:S(2)}) copy-start(s32[1,512]{1,0:T(1,128)} %param.13) | copy-start | bytes 6148
  0.7 20.9 %copy-start.7 = (f32[9,1024]{1,0:T(8,128)S(1)}, f32[9,1024]{1,0:T(8,128)}, u32[]{:S(2)}) copy-start(f32[9,1024]{1,0:T(8,128)} %param.15) | copy-start | bytes 110596
  2.2 80.4 %collective-permute-start.1 = (bf16[1,4,1024]{2,1,0:T(4,128)(2,1)}, bf16[1,4,1024]{2,1,0:T(4,128)(2,1)}, u32[]{:S(2)}, u32[]{:S(2)}) collective-permute-start(bf16[1,4,1024]{2,1,0:T(4,128)(2,1)} %get-tuple-element.113), channel_id=1, source_target_pairs={{1,0},{2,1},{3,2},{4,3},{5,4},{6,5},{7,6},{8,7},{9,8},{10,9},{11,1... | collective-permute-start | bytes 24584 | tf_op jit(solution)/shard_map/ppermute | solution.py:34
  7.3 76.0 %collective-permute-start = (bf16[1,4,1024]{2,1,0:T(4,128)(2,1)}, bf16[1,4,1024]{2,1,0:T(4,128)(2,1)S(1)}, u32[]{:S(2)}, u32[]{:S(2)}) collective-permute-start(bf16[1,4,1024]{2,1,0:T(4,128)(2,1)} %get-tuple-element.112), channel_id=1, source_target_pairs={{0,1},{1,2},{2,3},{3,4},{4,5},{5,6},{6,7},{7,8},{8,9},{9,10},{10,1... | collective-permute-start | bytes 24584 | tf_op jit(solution)/shard_map/ppermute | solution.py:31
  11.0 95.2 %all-to-all-start.1 = ((bf16[32,4,1024]{2,1,0:T(4,128)(2,1)}), bf16[32,4,1024]{2,1,0:T(4,128)(2,1)S(1)}, u32[]{:S(2)}, u32[]{:S(2)}) async-start(bf16[32,4,1024]{2,1,0:T(4,128)(2,1)} %reshape_squeeze.3), calls=%async_computation.1 | async-start | bytes 524288 | tf_op jit(solution)/shard_map/all_to_all | solution.py:135
  83.3 8.9 %copy-start.12 = (bf16[1024,3072]{1,0:T(8,128)(2,1)S(1)}, bf16[1024,3072]{1,0:T(8,128)(2,1)}, u32[]{:S(2)}) copy-start(bf16[1024,3072]{1,0:T(8,128)(2,1)} %param.17) | copy-start | bytes 18874372
  83.3 8.9 %copy-start.13 = (f32[1024]{0:T(1024)S(1)}, f32[1024]{0:T(1024)}, u32[]{:S(2)}) copy-start(f32[1024]{0:T(1024)} %param.16) | copy-start | bytes 12292
  91.7 4.5 %copy-start.2 = (bf16[512,1024]{1,0:T(8,128)(2,1)}, bf16[512,1024]{1,0:T(8,128)(2,1)S(1)}, u32[]{:S(2)}) copy-start(bf16[512,1024]{1,0:T(8,128)(2,1)S(1)} %get-tuple-element.107) | copy-start | bytes 3145732
  92.2 9.7 %copy-start.8 = (s32[1,64,1]{1,2,0:T(1,128)S(1)}, s32[1,64,1]{1,2,0:T(1,128)}, u32[]{:S(2)}) copy-start(s32[1,64,1]{1,2,0:T(1,128)} %param.14) | copy-start | bytes 772
  96.2 7.8 %copy-start.1 = (bf16[512,3072]{1,0:T(8,128)(2,1)}, bf16[512,3072]{1,0:T(8,128)(2,1)S(1)}, u32[]{:S(2)}) copy-start(bf16[512,3072]{1,0:T(8,128)(2,1)S(1)} %convolution_convert_fusion) | copy-start | bytes 9437188
  96.3 14.3 %collective-permute-start.2 = (bf16[96,2048]{1,0:T(8,128)(2,1)S(1)}, bf16[96,2048]{1,0:T(8,128)(2,1)S(1)}, u32[]{:S(2)}, u32[]{:S(2)}) collective-permute-start(bf16[96,2048]{1,0:T(8,128)(2,1)S(1)} %slice.152), channel_id=1, source_target_pairs={{0,1},{1,2},{2,3},{3,4},{4,5},{5,6},{6,7},{7,8},{8,9},{9,10},{10,1... | collective-permute-start | bytes 1179656 | tf_op jit(solution)/shard_map/ppermute | solution.py:42
  101.9 4.3 %copy-start.9 = (s32[64]{0:T(128)}, s32[64]{0:T(128)S(1)}, u32[]{:S(2)}) copy-start(s32[64]{0:T(128)S(1)} %multiply_add_fusion) | copy-start | bytes 772
  104.1 6.5 %collective-permute-start.3 = (bf16[32,2048]{1,0:T(8,128)(2,1)}, bf16[32,2048]{1,0:T(8,128)(2,1)S(1)}, u32[]{:S(2)}, u32[]{:S(2)}) collective-permute-start(bf16[32,2048]{1,0:T(8,128)(2,1)} %slice.154), channel_id=1, source_target_pairs={{1,0},{2,1},{3,2},{4,3},{5,4},{6,5},{7,6},{8,7},{9,8},{10,9},{11,1... | collective-permute-start | bytes 393224 | tf_op jit(solution)/shard_map/ppermute | solution.py:42
  116.3 6.8 %copy-start.5 = (pred[512,640]{1,0:T(8,128)(4,1)S(1)}, pred[512,640]{1,0:T(8,128)(4,1)}, u32[]{:S(2)}) copy-start(pred[512,640]{1,0:T(8,128)(4,1)} %compare_and_fusion) | copy-start | bytes 983044
  123.1 15.3 %copy-start.4 = (bf16[640,1024]{0,1:T(8,128)(2,1)S(1)}, bf16[640,1024]{0,1:T(8,128)(2,1)}, u32[]{:S(2)}) copy-start(bf16[640,1024]{0,1:T(8,128)(2,1)} %copy.16) | copy-start | bytes 3932164
  138.4 6.0 %copy-start.3 = (bf16[512,1024]{1,0:T(8,128)(2,1)S(1)}, bf16[512,1024]{1,0:T(8,128)(2,1)}, u32[]{:S(2)}) copy-start(bf16[512,1024]{1,0:T(8,128)(2,1)} %copy-done.2) | copy-start | bytes 3145732
  144.4 1.7 copy-start.10
  144.5 10.1 %copy-start.6 = (bf16[64,1024]{1,0:T(8,128)(2,1)S(1)}, bf16[64,1024]{1,0:T(8,128)(2,1)}, u32[]{:S(2)}) copy-start(bf16[64,1024]{1,0:T(8,128)(2,1)} %fusion.40) | copy-start | bytes 393220
  147.1 143.7 %all-to-all-start = ((bf16[32,4,1024]{2,1,0:T(4,128)(2,1)}), bf16[32,4,1024]{2,1,0:T(4,128)(2,1)S(1)}, u32[]{:S(2)}, u32[]{:S(2)}) async-start(bf16[32,4,1024]{2,1,0:T(4,128)(2,1)} %reshape.505), calls=%async_computation | async-start | bytes 524288 | tf_op jit(solution)/shard_map/all_to_all | solution.py:131
where the time goes:
time: 293 us; the launch traced here: 292 us
  blocking collectives  146 us (50%)
  local copies, waits for them, and re-layouts  34.7 us (12%)
  other arithmetic  34.6 us (12%)
  starting transfers between devices  30.6 us (10%)
  matrix products  22.7 us (8%)
  loops' own time  18.2 us (6%)
  waiting for transfers between devices  3.42 us (1%)
    psum x1, blocking collectives, shards(): grad_total = lax.psum(local_grad, ('grp', 'seq'))  133 us
    another operation x2, loops' own time, entering(): return lax.fori_loop(0, ahead, one, state)  18.2 us
    dynamic_slice x31, local copies, waits for them, and re-layouts, one(): return combine(state, lax.dynamic_index_in_dim(gathered, source, 0, False))  17.9 us
    sub x1, other arithmetic, shards(): expo = jnp.exp(scores - top)  15.3 us
    unnamed x1, blocking collectives  13.3 us
    all_to_all x1, starting transfers between devices, shards(): lax.all_to_all(cotangent[0].reshape(seq_count, slot_cap, width), 'seq', s...  8.45 us
    reduce_sum x1, other arithmetic, layer_norm(): centred = values - jnp.mean(values, axis=-1, keepdims=True)  8.42 us
    ppermute x2, starting transfers between devices, shifted(): return lax.ppermute(array, axis, pairs)  7.69 us
  transfers between devices with their start and end apart: 6, of which 1 were waited for; matrix products, arithmetic and copies ran while one was open for 18% of the time, Pallas kernels for 0%

commit v1 on v0

v1 whole, which is shorter than its diff:
```python
import jax
import jax.numpy as jnp
from jax import lax
from jax.experimental import pallas as pl
from jax.experimental.pallas import tpu as pltpu
from jax.sharding import PartitionSpec as P

HEADS = 8
BLOCK_LEN = 32
LEFT_BLOCKS = 2
SUB = 8
F = 512
D = 1024
LEFT = 112
RIGHT = 48
KV = 640
KOFF = 96
FAR = 1536
BIG = 1e6
F32 = jnp.float32
BF16 = jnp.bfloat16


def bounds(bg, t0, group_len, dprev, dnext):
    lanes = FAR + F + 128
    u = lax.broadcasted_iota(jnp.int32, (1, lanes), 1) - FAR
    at = u + t0
    mark = ((bg == 1) & (at >= 0)) | (at == group_len)
    uf = u.astype(F32)
    last = jnp.where(mark, uf, -BIG)
    early = jnp.max(last[:, : FAR - 128], axis=1, keepdims=True)
    near_last = last[:, FAR - 128 :]
    near_first = jnp.where(mark, uf, BIG)[:, FAR - 128 :]
    near = uf[:, FAR - 128 :]
    for c in range(KV // 128):
        t = (lax.broadcasted_iota(jnp.int32, (128, 1), 0) + (128 * c - KOFF)).astype(F32)
        before = near <= t
        start = jnp.max(jnp.where(before, near_last, -BIG), axis=1, keepdims=True)
        start = jnp.maximum(start, early)
        stop = jnp.min(jnp.where(before, BIG, near_first), axis=1, keepdims=True)
        dprev[128 * c : 128 * c + 128, :] = jnp.broadcast_to(t - start, (128, 128))
        dnext[128 * c : 128 * c + 128, :] = jnp.broadcast_to(stop - t, (128, 128))


def attention_bias(dprev, dnext, bias):
    for i in range(F // 128):
        rows = slice(KOFF + 128 * i, KOFF + 128 * i + 128)
        back = dprev[rows, :].astype(jnp.int32)
        ahead = dnext[rows, :].astype(jnp.int32)
        rem = back & (BLOCK_LEN - 1)
        low = -jnp.minimum(back, rem + LEFT_BLOCKS * BLOCK_LEN)
        high = jnp.minimum(ahead, BLOCK_LEN - rem)
        for half in range(2):
            delta = (
                lax.broadcasted_iota(jnp.int32, (128, 128), 1)
                - lax.broadcasted_iota(jnp.int32, (128, 128), 0)
                + (128 * half - KOFF)
            )
            ok = (delta >= low) & (delta < high)
            bias[i, :, 128 * half : 128 * half + 128] = jnp.where(ok, F32(0.0), F32(-1e30))


def conv_norm(xf, taps, gain, dprev, dnext, hid, nrm):
    step = 32
    tiles = D // 128

    def block(n, _):
        r0 = pl.multiple_of(n * step, step)
        back = dprev[pl.ds(r0, step), :]
        ahead = dnext[pl.ds(r0, step), :]
        keep = [back >= F32(4 - j) if j < 4 else ahead > F32(j - 4) for j in range(9)]
        hs = []
        total = jnp.zeros((step, 128), F32)
        for c in range(tiles):
            cols = slice(128 * c, 128 * c + 128)
            centre = xf[c, pl.ds(r0 + 16, step), :]
            acc = centre * taps[4:5, cols]
            for j in range(9):
                if j == 4:
                    continue
                term = xf[c, pl.ds(r0 + 12 + j, step), :] * taps[j : j + 1, cols]
                acc = acc + jnp.where(keep[j], term, F32(0.0))
            h16 = (centre + acc).astype(BF16)
            hid[pl.ds(r0, step), cols] = h16
            h = h16.astype(F32)
            hs.append(h)
            total = total + h
        mean = jnp.sum(total, axis=1, keepdims=True) * F32(1.0 / D)
        hs = [h - mean for h in hs]
        square = jnp.zeros((step, 128), F32)
        for h in hs:
            square = square + h * h
        var = jnp.sum(square, axis=1, keepdims=True) * F32(1.0 / D)
        scale = lax.rsqrt(var + F32(1e-5))
        for c in range(tiles):
            cols = slice(128 * c, 128 * c + 128)
            nrm[pl.ds(r0, step), cols] = (hs[c] * scale * gain[:, cols]).astype(BF16)
        return 0

    lax.fori_loop(0, KV // step, block, 0)


def attend(nrm, wqkv, bias, qs, ks, vs, attn):
    factor = F32(1.4426950408889634 / 128.0**0.5)

    def pair(hp, _):
        def cols(base):
            return pl.ds(pl.multiple_of(base + hp * 256, 256), 256)

        qs[...] = jnp.dot(
            nrm[KOFF : KOFF + F, :], wqkv[:, cols(0)], preferred_element_type=F32
        ).astype(BF16)
        ks[...] = jnp.dot(nrm[...], wqkv[:, cols(D)], preferred_element_type=F32).astype(BF16)
        vs[...] = jnp.dot(nrm[...], wqkv[:, cols(2 * D)], preferred_element_type=F32).astype(BF16)
        for hh in range(2):
            lanes = slice(128 * hh, 128 * hh + 128)
            for i in range(F // 128):
                q = qs[128 * i : 128 * i + 128, lanes]
                k = ks[128 * i : 128 * i + 256, lanes]
                v = vs[128 * i : 128 * i + 256, lanes]
                s = lax.dot_general(q, k, (((1,), (1,)), ((), ())), preferred_element_type=F32)
                s = s + bias[i]
                top = jnp.max(s, axis=1, keepdims=True)
                e = jnp.exp2((s - top) * factor)
                norm = F32(1.0) / jnp.sum(e, axis=1, keepdims=True)
                w = (e * norm).astype(BF16)
                o = jnp.dot(w, v, preferred_element_type=F32).astype(BF16)
                attn[
                    128 * i : 128 * i + 128,
                    pl.ds(pl.multiple_of(hp * 256 + 128 * hh, 128), 128),
                ] = o
        return 0

    lax.fori_loop(0, HEADS // 2, pair, 0)


def placement_of(owner):
    rows = owner.shape[0]
    lane = lax.broadcasted_iota(jnp.int32, (rows, 128), 1)
    hot = jnp.where(owner == lane, F32(1.0), F32(0.0))
    lower = jnp.where(
        lax.broadcasted_iota(jnp.int32, (rows, rows), 1)
        < lax.broadcasted_iota(jnp.int32, (rows, rows), 0),
        F32(1.0),
        F32(0.0),
    ).astype(BF16)
    before = jnp.dot(lower, hot.astype(BF16), preferred_element_type=F32)
    rank = jnp.sum(hot * before, axis=1, keepdims=True).astype(jnp.int32)
    slot = owner * 4 + rank
    return jnp.where(slot == lane, F32(1.0), F32(0.0)).astype(BF16)


def pool(hid, attn, wout):
    rows = F // SUB
    gather = jnp.where(
        lax.broadcasted_iota(jnp.int32, (rows, F), 1) >> 3
        == lax.broadcasted_iota(jnp.int32, (rows, F), 0),
        F32(1.0),
        F32(0.0),
    ).astype(BF16)
    asum = jnp.dot(gather, attn[...], preferred_element_type=F32)
    hsum = jnp.dot(gather, hid[KOFF : KOFF + F, :], preferred_element_type=F32)
    high = asum.astype(BF16)
    low = (asum - high.astype(F32)).astype(BF16)
    proj = jnp.dot(high, wout[...], preferred_element_type=F32)
    proj = proj + jnp.dot(low, wout[...], preferred_element_type=F32)
    pooled = ((hsum + proj) * F32(1.0 / SUB)).astype(BF16)
    return pooled, high, low


def local_kernel(
    x_hbm, bg_ref, owner_ref, taps_ref, gain_ref, wqkv_hbm, wout_hbm,
    out_ref, place_ref, a_ref,
    xb, xf, dprev, dnext, hid, nrm, qs, ks, vs, bias, attn, wqkv, wout, sems,
):
    cx = pltpu.make_async_copy(x_hbm, xb, sems.at[0])
    cq = pltpu.make_async_copy(wqkv_hbm, wqkv, sems.at[1])
    co = pltpu.make_async_copy(wout_hbm, wout, sems.at[2])
    cx.start()
    cq.start()
    co.start()
    t0 = lax.axis_index("seq") * F
    bounds(bg_ref[...], t0, F * lax.axis_size("seq"), dprev, dnext)
    attention_bias(dprev, dnext, bias)
    place = placement_of(owner_ref[...])
    place_ref[...] = place
    cx.wait()
    for c in range(D // 128):
        xf[c] = xb[:, 128 * c : 128 * c + 128].astype(F32)
    conv_norm(xf, taps_ref, gain_ref, dprev, dnext, hid, nrm)
    cq.wait()
    attend(nrm, wqkv, bias, qs, ks, vs, attn)
    co.wait()
    pooled, high, low = pool(hid, attn, wout)
    a_ref[0] = high
    a_ref[1] = low
    out_ref[...] = lax.dot_general(
        place, pooled, (((0,), (0,)), ((), ())), preferred_element_type=F32
    ).astype(BF16)


def shards(frames, begins, owner, conv_kernel, norm_gain, w_qkv, w_out, cotangent):
    n = lax.axis_size("seq")
    shift = lambda a, by: lax.ppermute(a, "seq", [(i, (i + by) % n) for i in range(n)])
    x = jnp.concatenate(
        [shift(frames[0, F - LEFT :], 1), frames[0], shift(frames[0, :RIGHT], -1)], axis=0
    )
    bg = jnp.concatenate(
        [shift(begins, 3), shift(begins, 2), shift(begins, 1), begins, shift(begins[:, :128], -1)],
        axis=1,
    )
    vm = pl.BlockSpec(memory_space=pltpu.VMEM)
    hbm = pl.BlockSpec(memory_space=pl.ANY)
    outgoing, place, asum = pl.pallas_call(
        local_kernel,
        out_shape=(
            jax.ShapeDtypeStruct((128, D), BF16),
            jax.ShapeDtypeStruct((64, 128), BF16),
            jax.ShapeDtypeStruct((2, 64, D), BF16),
        ),
        in_specs=[hbm, vm, vm, vm, vm, hbm, hbm],
        out_specs=(vm, vm, vm),
        scratch_shapes=[
            pltpu.VMEM((LEFT + F + RIGHT, D), BF16),
            pltpu.VMEM((8, LEFT + F + RIGHT, 128), F32),
            pltpu.VMEM((KV, 128), F32),
            pltpu.VMEM((KV, 128), F32),
            pltpu.VMEM((KV, D), BF16),
            pltpu.VMEM((KV, D), BF16),
            pltpu.VMEM((F, 256), BF16),
            pltpu.VMEM((KV, 256), BF16),
            pltpu.VMEM((KV, 256), BF16),
            pltpu.VMEM((4, 128, 256), F32),
            pltpu.VMEM((F, D), BF16),
            pltpu.VMEM((D, 3 * D), BF16),
            pltpu.VMEM((D, D), BF16),
            pltpu.SemaphoreType.DMA((3,)),
        ],
        compiler_params=pltpu.CompilerParams(vmem_limit_bytes=48 * 1024 * 1024),
        name="local",
    )(x, bg, owner[0], conv_kernel, norm_gain.reshape(1, D), w_qkv, w_out)
    incoming = lax.all_to_all(outgoing.reshape(n, 4, D), "seq", 0, 0, tiled=True)
    returned = lax.all_to_all(cotangent[0].reshape(n, 4, D), "seq", 0, 0, tiled=True)
    grads = jnp.dot(place, returned.reshape(128, D), preferred_element_type=F32).astype(BF16)
    dims = (((0,), (0,)), ((), ()))
    local = lax.dot_general(asum[0], grads, dims, preferred_element_type=F32)
    local = local + lax.dot_general(asum[1], grads, dims, preferred_element_type=F32)
    total = lax.psum(local * F32(1.0 / (8 * 128)), ("grp", "seq"))
    return incoming.reshape(1, 128, D), total.astype(BF16)


def solution(mesh):
    return jax.shard_map(
        shards,
        mesh=mesh,
        in_specs=(
            P("grp", "seq", None),
            P("grp", "seq"),
            P("grp", "seq", None),
            P(),
            P(),
            P(),
            P(),
            P("grp", "seq", None),
        ),
        out_specs=(P("grp", "seq", None), P()),
        check_vma=False,
    )
```

time: 293 us -> 197 us (0.67)
  other arithmetic: 34.6 us -> 1.36 us
  local copies, waits for them, and re-layouts: 34.7 us -> 7.41 us
  Pallas kernels: 0 us -> 23.9 us
  matrix products: 22.7 us -> 3.6 us
  loops' own time: 18.2 us -> 0 us
  blocking collectives: 146 us -> 133 us
  starting transfers between devices: 30.6 us -> 23 us
    pallas_call x0 -> x1, Pallas kernels: none -> 23.9 us  [shards(): pl.pallas_call(local_kernel, out_shape=(jax.ShapeDtypeStruct((128, D), BF...]
    dot_general x7 -> x3, matrix products: 22.7 us -> 3.6 us  [the longest x1 2.69 us: shards(): lax.dot_general(asum[1], grads, dims, preferred_element_type=F32)]
    another operation x2 -> x0, loops' own time: 18.2 us -> none  [entering(): return lax.fori_loop(0, ahead, one, state)]
    dynamic_slice x31 -> x0, local copies, waits for them, and re-layouts: 17.9 us -> none  [one(): return combine(state, lax.dynamic_index_in_dim(gathered, source, 0, False))]
    sub x2 -> x0, other arithmetic: 15.4 us -> none  [the longest x1 15.3 us: shards(): expo = jnp.exp(scores - top)]
    unnamed x1 -> x0, blocking collectives: 13.3 us -> none
    reduce_sum x3 -> x0, other arithmetic: 9.66 us -> none  [the longest x1 8.42 us: layer_norm(): centred = values - jnp.mean(values, axis=-1, keepdims=True)]
    unnamed x37 -> x10, local copies, waits for them, and re-layouts: 6.13 us -> 0.72 us
  transfers between devices with their start and end apart: 6 -> 8, of which waited for: 1 -> 1; matrix products, arithmetic and copies ran while one was open for 18% -> 6% of each run, Pallas kernels for 0% -> 12%
where the time goes in v1:
time: 197 us; the launch traced here: 196 us
  blocking collectives  133 us (68%)
  Pallas kernels  23.9 us (12%)
  starting transfers between devices  23 us (12%)
  local copies, waits for them, and re-layouts  7.41 us (4%)
  matrix products  3.6 us (2%)
  waiting for transfers between devices  3.23 us (2%)
    psum x1, blocking collectives, shards(): total = lax.psum(local * F32(1.0 / (8 * 128)), ('grp', 'seq'))  133 us
    pallas_call x1, Pallas kernels, shards(): pl.pallas_call(local_kernel, out_shape=(jax.ShapeDtypeStruct((128, D), BF...  23.9 us
    ppermute x6, starting transfers between devices, shards(): lax.ppermute(a, 'seq', [(i, (i + by) % n) for i in range(n)])  11 us
    all_to_all x1, starting transfers between devices, shards(): lax.all_to_all(outgoing.reshape(n, 4, D), 'seq', 0, 0, tiled=True)  8.15 us
  transfers between devices with their start and end apart: 8, of which 1 were waited for; matrix products, arithmetic and copies ran while one was open for 6% of the time, Pallas kernels for 12%

profile of v1, /device:TPU:1, one launch (start us, length us, event | category | flops | bytes accessed | tf_op | source)
XLA Modules:
  0.0 196.4 jit_solution(5748964323954793883)
XLA Ops:
  0.7 2.8 %collective-permute-start.4 = (s32[1,512]{1,0:T(1,128)}, s32[1,512]{1,0:T(1,128)S(1)}, u32[]{:S(2)}, u32[]{:S(2)}) collective-permute-start(s32[1,512]{1,0:T(1,128)} %param.9), channel_id=1, source_target_pairs={{0,1},{1,2},{2,3},{3,4},{4,5},{5,6},{6,7},{7,8},{8,9},{9,10},{10,1... | collective-permute-start | bytes 6152 | tf_op jit(solution)/shard_map/ppermute | solution.py:204
  3.4 1.3 collective-permute-start.3
  4.7 1.7 collective-permute-start.2
  6.4 0.7 slice.17
  7.1 0.0 collective-permute-start.5
  7.1 0.9 slice_bitcast_fusion.1
  8.0 3.6 %collective-permute-start.1 = (bf16[48,1024]{1,0:T(8,128)(2,1)S(1)}, bf16[48,1024]{1,0:T(8,128)(2,1)S(1)}, u32[]{:S(2)}, u32[]{:S(2)}) collective-permute-start(bf16[48,1024]{1,0:T(8,128)(2,1)S(1)} %slice_bitcast_fusion.1), channel_id=1, source_target_pairs={{0,31},{1,0},{2,1},{3,2},{4,3},{5,4},{6,5},{7,6},{8,7},{9,8},{10,9... | collective-permute-start | bytes 294920 | tf_op jit(solution)/shard_map/ppermute | solution.py:204
  11.6 1.8 reshape_squeeze.3
  13.3 3.8 %all-to-all-start.1 = ((bf16[32,4,1024]{2,1,0:T(4,128)(2,1)}), bf16[32,4,1024]{2,1,0:T(4,128)(2,1)S(1)}, u32[]{:S(2)}, u32[]{:S(2)}) async-start(bf16[32,4,1024]{2,1,0:T(4,128)(2,1)} %reshape_squeeze.3), calls=%async_computation.1 | async-start | bytes 524288 | tf_op jit(solution)/shard_map/all_to_all | solution.py:243
  17.2 1.0 slice_bitcast_fusion
  18.1 0.7 copy.10.owner_ref
  18.9 1.7 collective-permute-start
  20.6 0.7 constant_dynamic-update-slice_fusion.1
  21.3 3.2 %collective-permute-done = bf16[112,1024]{1,0:T(8,128)(2,1)S(1)} collective-permute-done((bf16[112,1024]{1,0:T(8,128)(2,1)S(1)}, bf16[112,1024]{1,0:T(8,128)(2,1)S(1)}, u32[]{:S(2)}, u32[]{:S(2)}) %collective-permute-start) | collective-permute-done | bytes 229408 | tf_op jit(solution)/shard_map/ppermute | solution.py:204
  24.5 1.4 pad_maximum_fusion.x_hbm
  25.9 23.9 %local.1 = (bf16[128,1024]{1,0:T(8,128)(2,1)S(1)}, bf16[64,128]{1,0:T(8,128)(2,1)S(1)}, bf16[2,64,1024]{2,1,0:T(8,128)(2,1)S(1)}) custom-call(bf16[672,1024]{1,0:T(8,128)(2,1)S(1)} %pad_maximum_fusion.x_hbm, s32[1,2176]{1,0:T(1,128)S(1)} %constant_dynamic-update-slice_fusion.bg_ref, s32[64,1]{1,0:T(8,128)S(1)} %copy.10.owner_ref, f32[9,1024]{1,0:T(8,128)S(1)} %copy-done.1, ...), custom_call_target="tpu_custom_call" | custom-call | tf_op jit(solution)/shard_map/local/pallas_call | solution.py:214
  49.9 0.8 reshape.17
  50.7 8.2 %all-to-all-start = ((bf16[32,4,1024]{2,1,0:T(4,128)(2,1)}), bf16[32,4,1024]{2,1,0:T(4,128)(2,1)S(1)}, u32[]{:S(2)}, u32[]{:S(2)}) async-start(bf16[32,4,1024]{2,1,0:T(4,128)(2,1)} %reshape.17), calls=%async_computation | async-start | bytes 524288 | tf_op jit(solution)/shard_map/all_to_all | solution.py:242
  58.8 0.1 reshape.19
  58.9 0.2 convolution_convert_fusion
  59.1 0.7 fusion.1
  59.8 2.7 %add_multiply_fusion = f32[1024,1024]{1,0:T(8,128)} fusion(f32[1024,1024]{1,0:T(8,128)S(1)} %fusion.1, bf16[64,1024]{1,0:T(8,128)(2,1)S(1)} %convolution_convert_fusion, bf16[2,64,1024]{2,1,0:T(8,128)(2,1)S(1)} %get-tuple-element.6), kind=kOutput, calls=%fused_computation | convolution fusion | flops 136314880 | bytes 8650752 | tf_op jit(solution)/shard_map/dot_general | solution.py:247
  62.5 133.1 %all-reduce.1 = bf16[1024,1024]{1,0:T(8,128)(2,1)} all-reduce(f32[1024,1024]{1,0:T(8,128)} %add_multiply_fusion), channel_id=1, replica_groups=mesh['grp'=8,'seq'=32] {'grp','seq'}, use_global_device_ids=true, to_apply=%region_0.0 | all-reduce | flops 1048576 | bytes 6291456 | tf_op jit(solution)/shard_map/psum | solution.py:248
  195.6 0.8 reshape.18
  (17 shorter events, 0.1 us)
Async XLA Ops:
  0.6 25.3 %copy-start = (bf16[1024,1024]{1,0:T(8,128)(2,1)S(1)}, bf16[1024,1024]{1,0:T(8,128)(2,1)}, u32[]{:S(2)}) copy-start(bf16[1024,1024]{1,0:T(8,128)(2,1)} %wout_hbm.1) | copy-start | bytes 6291460
  0.6 25.3 %copy-start.2 = (f32[1024]{0:T(1024)S(1)}, f32[1024]{0:T(1024)}, u32[]{:S(2)}) copy-start(f32[1024]{0:T(1024)} %param.12) | copy-start | bytes 12292
  0.7 25.3 %copy-start.1 = (f32[9,1024]{1,0:T(8,128)S(1)}, f32[9,1024]{1,0:T(8,128)}, u32[]{:S(2)}) copy-start(f32[9,1024]{1,0:T(8,128)} %taps_ref.1) | copy-start | bytes 110596
  0.7 20.0 %collective-permute-start.4 = (s32[1,512]{1,0:T(1,128)}, s32[1,512]{1,0:T(1,128)S(1)}, u32[]{:S(2)}, u32[]{:S(2)}) collective-permute-start(s32[1,512]{1,0:T(1,128)} %param.9), channel_id=1, source_target_pairs={{0,1},{1,2},{2,3},{3,4},{4,5},{5,6},{6,7},{7,8},{8,9},{9,10},{10,1... | collective-permute-start | bytes 6152 | tf_op jit(solution)/shard_map/ppermute | solution.py:204
  3.4 17.2 %collective-permute-start.3 = (s32[1,512]{1,0:T(1,128)}, s32[1,512]{1,0:T(1,128)S(1)}, u32[]{:S(2)}, u32[]{:S(2)}) collective-permute-start(s32[1,512]{1,0:T(1,128)} %param.9), channel_id=1, source_target_pairs={{0,2},{1,3},{2,4},{3,5},{4,6},{5,7},{6,8},{7,9},{8,10},{9,11},{10,... | collective-permute-start | bytes 6152 | tf_op jit(solution)/shard_map/ppermute | solution.py:204
  4.7 14.2 %collective-permute-start.2 = (s32[1,512]{1,0:T(1,128)}, s32[1,512]{1,0:T(1,128)S(1)}, u32[]{:S(2)}, u32[]{:S(2)}) collective-permute-start(s32[1,512]{1,0:T(1,128)} %param.9), channel_id=1, source_target_pairs={{0,3},{1,4},{2,5},{3,6},{4,7},{5,8},{6,9},{7,10},{8,11},{9,12},{10... | collective-permute-start | bytes 6152 | tf_op jit(solution)/shard_map/ppermute | solution.py:204
  7.1 14.2 %collective-permute-start.5 = (s32[1,128]{1,0:T(1,128)S(1)}, s32[1,128]{1,0:T(1,128)S(1)}, u32[]{:S(2)}, u32[]{:S(2)}) collective-permute-start(s32[1,128]{1,0:T(1,128)S(1)} %slice.17), channel_id=1, source_target_pairs={{0,31},{1,0},{2,1},{3,2},{4,3},{5,4},{6,5},{7,6},{8,7},{9,8},{10,9... | collective-permute-start | bytes 1544 | tf_op jit(solution)/shard_map/ppermute | solution.py:204
  8.0 13.3 %collective-permute-start.1 = (bf16[48,1024]{1,0:T(8,128)(2,1)S(1)}, bf16[48,1024]{1,0:T(8,128)(2,1)S(1)}, u32[]{:S(2)}, u32[]{:S(2)}) collective-permute-start(bf16[48,1024]{1,0:T(8,128)(2,1)S(1)} %slice_bitcast_fusion.1), channel_id=1, source_target_pairs={{0,31},{1,0},{2,1},{3,2},{4,3},{5,4},{6,5},{7,6},{8,7},{9,8},{10,9... | collective-permute-start | bytes 294920 | tf_op jit(solution)/shard_map/ppermute | solution.py:204
  13.3 37.4 %all-to-all-start.1 = ((bf16[32,4,1024]{2,1,0:T(4,128)(2,1)}), bf16[32,4,1024]{2,1,0:T(4,128)(2,1)S(1)}, u32[]{:S(2)}, u32[]{:S(2)}) async-start(bf16[32,4,1024]{2,1,0:T(4,128)(2,1)} %reshape_squeeze.3), calls=%async_computation.1 | async-start | bytes 524288 | tf_op jit(solution)/shard_map/all_to_all | solution.py:243
  18.9 5.7 %collective-permute-start = (bf16[112,1024]{1,0:T(8,128)(2,1)S(1)}, bf16[112,1024]{1,0:T(8,128)(2,1)S(1)}, u32[]{:S(2)}, u32[]{:S(2)}) collective-permute-start(bf16[112,1024]{1,0:T(8,128)(2,1)S(1)} %slice_bitcast_fusion), channel_id=1, source_target_pairs={{0,1},{1,2},{2,3},{3,4},{4,5},{5,6},{6,7},{7,8},{8,9},{9,10},{10,1... | collective-permute-start | bytes 688136 | tf_op jit(solution)/shard_map/ppermute | solution.py:204
  50.7 144.9 %all-to-all-start = ((bf16[32,4,1024]{2,1,0:T(4,128)(2,1)}), bf16[32,4,1024]{2,1,0:T(4,128)(2,1)S(1)}, u32[]{:S(2)}, u32[]{:S(2)}) async-start(bf16[32,4,1024]{2,1,0:T(4,128)(2,1)} %reshape.17), calls=%async_computation | async-start | bytes 524288 | tf_op jit(solution)/shard_map/all_to_all | solution.py:242

commit v2 on v1

--- a/solution.py
+++ b/solution.py
@@ -19,6 +19,12 @@
 BIG = 1e6
 F32 = jnp.float32
 BF16 = jnp.bfloat16
+MESH = pl.DeviceIdType.MESH
+N_SEQ = 32
+N_GRP = 8
+N_X = 4
+N_Y = 4
+GROUP = 8
 
 
 def bounds(bg, t0, group_len, dprev, dnext):
@@ -150,7 +156,142 @@
     return jnp.where(slot == lane, F32(1.0), F32(0.0)).astype(BF16)
 
 
-def pool(hid, attn, wout):
+def remote(src, dst, sends, recvs, index, target):
+    return pltpu.make_async_remote_copy(
+        src_ref=src,
+        dst_ref=dst,
+        send_sem=sends.at[index],
+        recv_sem=recvs.at[index],
+        device_id=target,
+        device_id_type=MESH,
+    )
+
+
+def each(count, body):
+    def one(k, _):
+        body(k)
+        return 0
+
+    lax.fori_loop(1, count, one, 0)
+
+
+def to_slots(value, wide, slots):
+    for c in range(D // 128):
+        wide[pl.ds(c, 128, stride=8), :] = value[:, 128 * c : 128 * c + 128].astype(F32)
+    for o in range(N_SEQ):
+        slots[o] = wide[32 * o : 32 * o + 32, :].astype(BF16)
+
+
+def from_slots(slots, wide):
+    for o in range(N_SEQ):
+        wide[32 * o : 32 * o + 32, :] = slots[o].astype(F32)
+    return [wide[pl.ds(c, 128, stride=8), :].astype(BF16) for c in range(D // 128)]
+
+
+def whole_kernel(
+    frames, begins, owner, taps, gain, wqkv_hbm, wout_hbm, cot_hbm,
+    audio, fin,
+    xb, xf, bgs, dprev, dnext, hid, nrm, qs, ks, vs, bias, attn, wqkv, wout,
+    cotv, cots, back, wide, gall, asp, aall, part, xr, quarter, zr, aout,
+    local_sems, halo_s, halo_r, cot_s, cot_r, g_s, g_r, a_s, a_r, x_s, x_r, z_s, z_r,
+    t_s, t_r, m_s, m_r, h0_s, h0_r, h1_s, h1_r, p0_s, p0_r, p1_s, p1_r, c_s, c_r,
+):
+    z = lax.axis_index("grp")
+    s = lax.axis_index("seq")
+    x = s // GROUP
+    j = s % GROUP
+    y = j // 2
+    c = j % 2
+
+    def seq(k):
+        return {"seq": (s + k) % N_SEQ}
+
+    def grp(k):
+        return {"grp": (z + k) % N_GRP}
+
+    def in_group(k):
+        return {"seq": x * GROUP + (j + k) % GROUP}
+
+    def along_x(k):
+        return {"seq": (x + k) % N_X * GROUP + j}
+
+    def along_y(k):
+        return {"seq": x * GROUP + (y + k) % N_Y * 2 + c}
+
+    other_core = {"seq": x * GROUP + y * 2 + (1 - c)}
+
+    barrier = pltpu.get_barrier_semaphore()
+
+    def greet(target):
+        pl.semaphore_signal(barrier, inc=1, device_id=target, device_id_type=MESH)
+
+    each(N_SEQ, lambda k: greet(seq(k)))
+    each(N_GRP, lambda k: greet(grp(k)))
+
+    loads = [
+        pltpu.make_async_copy(cot_hbm.at[0], cotv, local_sems.at[0]),
+        pltpu.make_async_copy(begins, bgs.at[3], local_sems.at[1]),
+        pltpu.make_async_copy(frames.at[0], xb.at[pl.ds(LEFT, F)], local_sems.at[2]),
+        pltpu.make_async_copy(wqkv_hbm, wqkv, local_sems.at[3]),
+        pltpu.make_async_copy(wout_hbm, wout, local_sems.at[4]),
+    ]
+    for copy in loads:
+        copy.start()
+    loads[0].wait()
+    to_slots(cotv[...], wide, cots)
+    place = placement_of(owner[...])
+
+    pl.semaphore_wait(barrier, N_SEQ - 1 + N_GRP - 1)
+
+    halo = [
+        remote(frames.at[0, pl.ds(F - LEFT, LEFT)], xb.at[pl.ds(0, LEFT)], halo_s, halo_r, 0, seq(1)),
+        remote(frames.at[0, pl.ds(0, RIGHT)], xb.at[pl.ds(LEFT + F, RIGHT)], halo_s, halo_r, 1, seq(N_SEQ - 1)),
+        remote(begins, bgs.at[2], halo_s, halo_r, 2, seq(1)),
+        remote(begins, bgs.at[1], halo_s, halo_r, 3, seq(2)),
+        remote(begins, bgs.at[0], halo_s, halo_r, 4, seq(3)),
+        remote(begins, bgs.at[4], halo_s, halo_r, 5, seq(N_SEQ - 1)),
+    ]
+    for copy in halo[2:] + halo[:2]:
+        copy.start()
+
+    def send_cot(k):
+        remote(cots.at[(s + k) % N_SEQ], back.at[s], cot_s, cot_r, k, seq(k)).start()
+
+    each(N_SEQ, send_cot)
+    back[s] = cots[s]
+
+    loads[1].wait()
+    for copy in halo[2:]:
+        copy.wait_recv()
+    marks = jnp.concatenate([bgs[0], bgs[1], bgs[2], bgs[3], bgs[4][:, :128]], axis=1)
+    bounds(marks, s * F, F * N_SEQ, dprev, dnext)
+    attention_bias(dprev, dnext, bias)
+    loads[2].wait()
+    for copy in halo[:2]:
+        copy.wait_recv()
+    for tile in range(D // 128):
+        xf[tile] = xb[:, 128 * tile : 128 * tile + 128].astype(F32)
+    conv_norm(xf, taps, gain, dprev, dnext, hid, nrm)
+
+    def got_cot(k):
+        source = (s + N_SEQ - k) % N_SEQ
+        remote(back.at[source], back.at[source], cot_s, cot_r, k, seq(k)).wait_recv()
+
+    each(N_SEQ, got_cot)
+    mine = pl.ds(pl.multiple_of(j * 64, 64), 64)
+    returned = from_slots(back, wide)
+    for tile in range(D // 128):
+        gall[mine, 128 * tile : 128 * tile + 128] = jnp.dot(
+            place, returned[tile], preferred_element_type=F32
+        ).astype(BF16)
+
+    def copy_g(k):
+        return remote(gall.at[mine], gall.at[mine], g_s, g_r, k, in_group(k))
+
+    each(GROUP, lambda k: copy_g(k).start())
+
+    loads[3].wait()
+    attend(nrm, wqkv, bias, qs, ks, vs, attn)
     rows = F // SUB
     gather = jnp.where(
         lax.broadcasted_iota(jnp.int32, (rows, F), 1) >> 3
@@ -159,70 +300,170 @@
         F32(0.0),
     ).astype(BF16)
     asum = jnp.dot(gather, attn[...], preferred_element_type=F32)
-    hsum = jnp.dot(gather, hid[KOFF : KOFF + F, :], preferred_element_type=F32)
     high = asum.astype(BF16)
     low = (asum - high.astype(F32)).astype(BF16)
+    for h in range(HEADS):
+        asp[h, 0] = high[:, 128 * h : 128 * h + 128]
+        asp[h, 1] = low[:, 128 * h : 128 * h + 128]
+
+    def copy_a(k):
+        return remote(asp.at[(j + k) % GROUP], aall.at[:, mine, :], a_s, a_r, k, in_group(k))
+
+    each(GROUP, lambda k: copy_a(k).start())
+    aall[:, mine, :] = asp[j]
+
+    loads[4].wait()
+    hsum = jnp.dot(gather, hid[KOFF : KOFF + F, :], preferred_element_type=F32)
     proj = jnp.dot(high, wout[...], preferred_element_type=F32)
     proj = proj + jnp.dot(low, wout[...], preferred_element_type=F32)
     pooled = ((hsum + proj) * F32(1.0 / SUB)).astype(BF16)
-    return pooled, high, low
-
-
-def local_kernel(
-    x_hbm, bg_ref, owner_ref, taps_ref, gain_ref, wqkv_hbm, wout_hbm,
-    out_ref, place_ref, a_ref,
-    xb, xf, dprev, dnext, hid, nrm, qs, ks, vs, bias, attn, wqkv, wout, sems,
-):
-    cx = pltpu.make_async_copy(x_hbm, xb, sems.at[0])
-    cq = pltpu.make_async_copy(wqkv_hbm, wqkv, sems.at[1])
-    co = pltpu.make_async_copy(wout_hbm, wout, sems.at[2])
-    cx.start()
-    cq.start()
-    co.start()
-    t0 = lax.axis_index("seq") * F
-    bounds(bg_ref[...], t0, F * lax.axis_size("seq"), dprev, dnext)
-    attention_bias(dprev, dnext, bias)
-    place = placement_of(owner_ref[...])
-    place_ref[...] = place
-    cx.wait()
-    for c in range(D // 128):
-        xf[c] = xb[:, 128 * c : 128 * c + 128].astype(F32)
-    conv_norm(xf, taps_ref, gain_ref, dprev, dnext, hid, nrm)
-    cq.wait()
-    attend(nrm, wqkv, bias, qs, ks, vs, attn)
-    co.wait()
-    pooled, high, low = pool(hid, attn, wout)
-    a_ref[0] = high
-    a_ref[1] = low
-    out_ref[...] = lax.dot_general(
-        place, pooled, (((0,), (0,)), ((), ())), preferred_element_type=F32
-    ).astype(BF16)
+    dims = (((0,), (0,)), ((), ()))
+    outgoing = lax.dot_general(place, pooled, dims, preferred_element_type=F32)
+    to_slots(outgoing, wide, aout)
+
+    def copy_audio(k):
+        return remote(aout.at[(s + k) % N_SEQ], audio.at[s], m_s, m_r, k, seq(k))
+
+    each(N_SEQ, lambda k: copy_audio(k).start())
+    audio[s] = aout[s]
+
+    each(GROUP, lambda k: copy_g(k).wait_recv())
+    each(GROUP, lambda k: copy_a(k).wait_recv())
+    part[...] = lax.dot_general(aall[0], gall[...], dims, preferred_element_type=F32)
+    part[...] += lax.dot_general(aall[1], gall[...], dims, preferred_element_type=F32)
+
+    def rows_of(place_x):
+        return pl.ds(pl.multiple_of(place_x * 32, 32), 32)
+
+    def copy_x(k):
+        return remote(part.at[rows_of((x + k) % N_X)], xr.at[k], x_s, x_r, k, along_x(k))
+
+    for k in range(1, N_X):
+        copy_x(k).start()
+    for k in range(1, N_X):
+        copy_x(k).wait_recv()
+    total = part[rows_of(x), :] + xr[1] + xr[2] + xr[3]
+    for tile in range(N_GRP):
+        quarter[tile] = total[:, 128 * tile : 128 * tile + 128]
+
+    def copy_z(k):
+        return remote(quarter.at[(z + k) % N_GRP], zr.at[k], z_s, z_r, k, grp(k))
+
+    for k in range(1, N_GRP):
+        copy_z(k).start()
+    for k in range(1, N_GRP):
+        copy_z(k).wait_recv()
+    tile_sum = quarter[z]
+    for k in range(1, N_GRP):
+        tile_sum = tile_sum + zr[k]
+    own_cols = pl.ds(pl.multiple_of(z * 128, 128), 128)
+    fin[y, c, x, :, own_cols] = (tile_sum * F32(1.0 / (128 * SUB))).astype(BF16)
+
+    def copy_t(k):
+        tile = fin.at[y, c, x, :, own_cols]
+        return remote(tile, tile, t_s, t_r, k, grp(k))
+
+    for k in range(1, N_GRP):
+        copy_t(k).start()
+    for k in range(1, N_GRP):
+        copy_t(k).wait_recv()
+
+    first, second = pl.ds(0, D // 2), pl.ds(D // 2, D // 2)
+
+    def copy_h0(k):
+        block = fin.at[y, c, x, :, first]
+        return remote(block, block, h0_s, h0_r, k, along_x(k))
+
+    def copy_h1(k):
+        block = fin.at[y, c, x, :, second]
+        return remote(block, block, h1_s, h1_r, k, along_y(k))
+
+    def copy_p0(k):
+        block = fin.at[y, c, :, :, first]
+        return remote(block, block, p0_s, p0_r, k, along_y(k))
+
+    def copy_p1(k):
+        block = fin.at[:, c, x, :, second]
+        return remote(block, block, p1_s, p1_r, k, along_x(k))
+
+    def copy_c0(k):
+        block = fin.at[(y + N_Y - k) % N_Y, c, :, :, first]
+        return remote(block, block, c_s, c_r, k, other_core)
+
+    def copy_c1(k):
+        block = fin.at[:, c, (x + N_X - k) % N_X, :, second]
+        return remote(block, block, c_s, c_r, N_Y + k, other_core)
+
+    for k in range(1, N_X):
+        copy_h0(k).start()
+        copy_h1(k).start()
+    for k in range(1, N_X):
+        copy_h0(k).wait_recv()
+    for k in range(1, N_Y):
+        copy_p0(k).start()
+    copy_c0(0).start()
+    for k in range(1, N_Y):
+        copy_h1(k).wait_recv()
+    for k in range(1, N_X):
+        copy_p1(k).start()
+    copy_c1(0).start()
+    for k in (1, 3, 2):
+        copy_p0(k).wait_recv()
+        copy_c0(k).start()
+        copy_p1(k).wait_recv()
+        copy_c1(k).start()
+    for k in range(N_Y):
+        copy_c0(k).wait_recv()
+        copy_c1(k).wait_recv()
+
+    def got_audio(k):
+        source = (s + N_SEQ - k) % N_SEQ
+        remote(audio.at[source], audio.at[source], m_s, m_r, k, seq(k)).wait_recv()
+
+    each(N_SEQ, got_audio)
+    for copy in halo:
+        copy.wait_send()
+
+    def sent(k):
+        remote(cots.at[(s + k) % N_SEQ], back.at[s], cot_s, cot_r, k, seq(k)).wait_send()
+        copy_audio(k).wait_send()
+
+    each(N_SEQ, sent)
+
+    def sent_group(k):
+        copy_g(k).wait_send()
+        copy_a(k).wait_send()
+        copy_z(k).wait_send()
+        copy_t(k).wait_send()
+
+    each(GROUP, sent_group)
+    for k in range(1, N_X):
+        copy_x(k).wait_send()
+        copy_h0(k).wait_send()
+        copy_h1(k).wait_send()
+        copy_p0(k).wait_send()
+        copy_p1(k).wait_send()
+    for k in range(N_Y):
+        copy_c0(k).wait_send()
+        copy_c1(k).wait_send()
 
 
 def shards(frames, begins, owner, conv_kernel, norm_gain, w_qkv, w_out, cotangent):
-    n = lax.axis_size("seq")
-    shift = lambda a, by: lax.ppermute(a, "seq", [(i, (i + by) % n) for i in range(n)])
-    x = jnp.concatenate(
-        [shift(frames[0, F - LEFT :], 1), frames[0], shift(frames[0, :RIGHT], -1)], axis=0
-    )
-    bg = jnp.concatenate(
-        [shift(begins, 3), shift(begins, 2), shift(begins, 1), begins, shift(begins[:, :128], -1)],
-        axis=1,
-    )
     vm = pl.BlockSpec(memory_space=pltpu.VMEM)
     hbm = pl.BlockSpec(memory_space=pl.ANY)
-    outgoing, place, asum = pl.pallas_call(
-        local_kernel,
+    dma = pltpu.SemaphoreType.DMA
+    audio, grad = pl.pallas_call(
+        whole_kernel,
         out_shape=(
-            jax.ShapeDtypeStruct((128, D), BF16),
-            jax.ShapeDtypeStruct((64, 128), BF16),
-            jax.ShapeDtypeStruct((2, 64, D), BF16),
+            jax.ShapeDtypeStruct((N_SEQ, 32, 128), BF16),
+            jax.ShapeDtypeStruct((N_Y, 2, N_X, 32, D), BF16),
         ),
-        in_specs=[hbm, vm, vm, vm, vm, hbm, hbm],
-        out_specs=(vm, vm, vm),
+        in_specs=[hbm, hbm, vm, vm, vm, hbm, hbm, hbm],
+        out_specs=(vm, vm),
         scratch_shapes=[
             pltpu.VMEM((LEFT + F + RIGHT, D), BF16),
             pltpu.VMEM((8, LEFT + F + RIGHT, 128), F32),
+            pltpu.VMEM((5, 1, F), jnp.int32),
             pltpu.VMEM((KV, 128), F32),
             pltpu.VMEM((KV, 128), F32),
             pltpu.VMEM((KV, D), BF16),
@@ -234,19 +475,39 @@
             pltpu.VMEM((F, D), BF16),
             pltpu.VMEM((D, 3 * D), BF16),
             pltpu.VMEM((D, D), BF16),
-            pltpu.SemaphoreType.DMA((3,)),
+            pltpu.VMEM((128, D), BF16),
+            pltpu.VMEM((N_SEQ, 32, 128), BF16),
+            pltpu.VMEM((N_SEQ, 32, 128), BF16),
+            pltpu.VMEM((1024, 128), F32),
+            pltpu.VMEM((512, D), BF16),
+            pltpu.VMEM((HEADS, 2, 64, 128), BF16),
+            pltpu.VMEM((2, 512, 128), BF16),
+            pltpu.VMEM((128, D), F32),
+            pltpu.VMEM((N_X, 32, D), F32),
+            pltpu.VMEM((N_GRP, 32, 128), F32),
+            pltpu.VMEM((N_GRP, 32, 128), F32),
+            pltpu.VMEM((N_SEQ, 32, 128), BF16),
+            dma((5,)),
+            dma((6,)), dma((6,)),
+            dma((N_SEQ,)), dma((N_SEQ,)),
+            dma((GROUP,)), dma((GROUP,)),
+            dma((GROUP,)), dma((GROUP,)),
+            dma((N_X,)), dma((N_X,)),
+            dma((N_GRP,)), dma((N_GRP,)),
+            dma((N_GRP,)), dma((N_GRP,)),
+            dma((N_SEQ,)), dma((N_SEQ,)),
+            dma((N_X,)), dma((N_X,)),
+            dma((N_Y,)), dma((N_Y,)),
+            dma((N_Y,)), dma((N_Y,)),
+            dma((N_X,)), dma((N_X,)),
+            dma((2 * N_Y,)), dma((2 * N_Y,)),
         ],
-        compiler_params=pltpu.CompilerParams(vmem_limit_bytes=48 * 1024 * 1024),
-        name="local",
-    )(x, bg, owner[0], conv_kernel, norm_gain.reshape(1, D), w_qkv, w_out)
-    incoming = lax.all_to_all(outgoing.reshape(n, 4, D), "seq", 0, 0, tiled=True)
-    returned = lax.all_to_all(cotangent[0].reshape(n, 4, D), "seq", 0, 0, tiled=True)
-    grads = jnp.dot(place, returned.reshape(128, D), preferred_element_type=F32).astype(BF16)
-    dims = (((0,), (0,)), ((), ()))
-    local = lax.dot_general(asum[0], grads, dims, preferred_element_type=F32)
-    local = local + lax.dot_general(asum[1], grads, dims, preferred_element_type=F32)
-    total = lax.psum(local * F32(1.0 / (8 * 128)), ("grp", "seq"))
-    return incoming.reshape(1, 128, D), total.astype(BF16)
+        compiler_params=pltpu.CompilerParams(
+            vmem_limit_bytes=48 * 1024 * 1024, collective_id=0, has_side_effects=True
+        ),
+        name="whole",
+    )(frames, begins, owner[0], conv_kernel, norm_gain.reshape(1, D), w_qkv, w_out, cotangent)
+    return audio.reshape(1, 128, D), grad.reshape(D, D)
 
 
 def solution(mesh):

time: 197 us -> 91.9 us (0.47)
  blocking collectives: 133 us -> 0 us
  Pallas kernels: 23.9 us -> 82.1 us
  starting transfers between devices: 23 us -> 0 us
  matrix products: 3.6 us -> 0 us
  waiting for transfers between devices: 3.23 us -> 0 us
    psum x1 -> x0, blocking collectives: 133 us -> none  [shards(): total = lax.psum(local * F32(1.0 / (8 * 128)), ('grp', 'seq'))]
    pallas_call x1, Pallas kernels: 23.9 us -> 82.1 us  [shards(): pl.pallas_call(whole_kernel, out_shape=(jax.ShapeDtypeStruct((N_SEQ, 32,...]
    all_to_all x2 -> x0, starting transfers between devices: 12 us -> none  [the longest x1 8.15 us: shards(): lax.all_to_all(outgoing.reshape(n, 4, D), 'seq', 0, 0, tiled=True)]
    ppermute x6 -> x0, starting transfers between devices: 11 us -> none  [shards(): lax.ppermute(a, 'seq', [(i, (i + by) % n) for i in range(n)])]
    unnamed x10 -> x13, local copies, waits for them, and re-layouts: 0.72 us -> 7.29 us
    dot_general x3 -> x0, matrix products: 3.6 us -> none  [the longest x1 2.69 us: shards(): lax.dot_general(asum[1], grads, dims, preferred_element_type=F32)]
    ppermute x6 -> x0, waiting for transfers between devices: 3.22 us -> none  [shards(): lax.ppermute(a, 'seq', [(i, (i + by) % n) for i in range(n)])]
  transfers between devices with their start and end apart: 8 -> 0, of which waited for: 1 -> 0; matrix products, arithmetic and copies ran while one was open for 6% -> 0% of each run, Pallas kernels for 12% -> 0%
where the time goes in v2:
time: 91.9 us; the launch traced here: 91.6 us
  Pallas kernels  82.1 us (89%)
  local copies, waits for them, and re-layouts  8.85 us (10%)
    pallas_call x1, Pallas kernels, shards(): pl.pallas_call(whole_kernel, out_shape=(jax.ShapeDtypeStruct((N_SEQ, 32,...  82.1 us
    unnamed x13, local copies, waits for them, and re-layouts  7.29 us

profile of v2, /device:TPU:1, one launch (start us, length us, event | category | flops | bytes accessed | tf_op | source)
XLA Modules:
  0.0 91.6 jit_solution(8996956304511349434)
XLA Ops:
  0.6 0.7 copy.10.owner
  1.4 0.0 copy-start
  1.4 1.6 %copy-done = bf16[1024,1024]{1,0:T(8,128)(2,1)S(1)} copy-done((bf16[1024,1024]{1,0:T(8,128)(2,1)S(1)}, bf16[1024,1024]{1,0:T(8,128)(2,1)}, u32[]{:S(2)}) %copy-start) | copy-done | bytes 2097176
  3.0 0.0 copy-start.1
  3.0 1.2 %copy-done.1 = bf16[1,512,1024]{2,1,0:T(8,128)(2,1)S(1)} copy-done((bf16[1,512,1024]{2,1,0:T(8,128)(2,1)S(1)}, bf16[1,512,1024]{2,1,0:T(8,128)(2,1)}, u32[]{:S(2)}) %copy-start.1) | copy-done | bytes 1048600
  4.2 0.0 copy-start.2
  4.2 0.9 %copy-done.2 = bf16[1,128,1024]{2,1,0:T(8,128)(2,1)S(1)} copy-done((bf16[1,128,1024]{2,1,0:T(8,128)(2,1)S(1)}, bf16[1,128,1024]{2,1,0:T(8,128)(2,1)}, u32[]{:S(2)}) %copy-start.2) | copy-done | bytes 262168
  5.1 0.0 copy-start.3
  5.1 0.8 copy-done.3
  6.0 0.0 copy-start.4
  6.0 0.7 copy-done.4
  6.7 0.0 copy-start.5
  6.7 0.7 copy-done.5
  7.4 82.1 %whole.1 = (bf16[32,32,128]{2,1,0:T(8,128)(2,1)S(1)}, bf16[4,2,4,32,1024]{4,3,2,1,0:T(8,128)(2,1)S(1)}) custom-call(bf16[1,512,1024]{2,1,0:T(8,128)(2,1)S(1)} %copy-done.1, s32[1,512]{1,0:T(1,128)S(1)} %copy-done.5, s32[64,1]{1,0:T(8,128)S(1)} %copy.10.owner, f32[9,1024]{1,0:T(8,128)S(1)} %copy-done.3, f32[1,1024]{1,0:T(1,128)S(1)} %bitcast.4, ...), custom_call_target="tpu_custom_call" | custom-call | tf_op jit(solution)/shard_map/whole/pallas_call | solution.py:455
  89.5 0.8 reshape.14
  90.3 1.3 %copy.12 = bf16[1024,1024]{1,0:T(8,128)(2,1)} copy(bf16[1024,1024]{1,0:T(8,128)(2,1)S(1)} %bitcast.3) | data formatting | bytes 4194304
Async XLA Ops:
  1.4 1.6 %copy-start = (bf16[1024,1024]{1,0:T(8,128)(2,1)S(1)}, bf16[1024,1024]{1,0:T(8,128)(2,1)}, u32[]{:S(2)}) copy-start(bf16[1024,1024]{1,0:T(8,128)(2,1)} %wout_hbm.1) | copy-start | bytes 6291460
  3.0 1.2 %copy-start.1 = (bf16[1,512,1024]{2,1,0:T(8,128)(2,1)S(1)}, bf16[1,512,1024]{2,1,0:T(8,128)(2,1)}, u32[]{:S(2)}) copy-start(bf16[1,512,1024]{2,1,0:T(8,128)(2,1)} %frames.1) | copy-start | bytes 3145732
  4.2 0.9 %copy-start.2 = (bf16[1,128,1024]{2,1,0:T(8,128)(2,1)S(1)}, bf16[1,128,1024]{2,1,0:T(8,128)(2,1)}, u32[]{:S(2)}) copy-start(bf16[1,128,1024]{2,1,0:T(8,128)(2,1)} %cot_hbm.1) | copy-start | bytes 786436
  5.1 0.8 copy-start.3
  6.0 0.7 copy-start.4
  6.7 0.7 copy-start.5

commit v3 on v2

v3 whole, which is shorter than its diff:
```python
import jax
import jax.numpy as jnp
from jax import lax
from jax.experimental import pallas as pl
from jax.experimental.pallas import tpu as pltpu
from jax.sharding import PartitionSpec as P

HEADS = 8
BLOCK_LEN = 32
LEFT_BLOCKS = 2
SUB = 8
F = 512
D = 1024
LEFT = 112
RIGHT = 48
KV = 640
KOFF = 96
FAR = 1536
BIG = 1e6
F32 = jnp.float32
BF16 = jnp.bfloat16
MESH = pl.DeviceIdType.MESH
N_SEQ = 32
N_GRP = 8
N_X = 4
N_Y = 4
GROUP = 8


def bounds(bg, t0, group_len, dprev, dnext):
    lanes = FAR + F + 128
    u = lax.broadcasted_iota(jnp.int32, (1, lanes), 1) - FAR
    at = u + t0
    mark = ((bg == 1) & (at >= 0)) | (at == group_len)
    uf = u.astype(F32)
    last = jnp.where(mark, uf, -BIG)
    first = jnp.where(mark, uf, BIG)
    for c in range(KV // 128):
        window = slice(FAR - 128 + 128 * c, FAR + 128 + 128 * c)
        early = jnp.max(last[:, : FAR - 128 + 128 * c], axis=1, keepdims=True)
        t = (lax.broadcasted_iota(jnp.int32, (128, 1), 0) + (128 * c - KOFF)).astype(F32)
        before = uf[:, window] <= t
        start = jnp.max(jnp.where(before, last[:, window], -BIG), axis=1, keepdims=True)
        start = jnp.maximum(start, early)
        stop = jnp.min(jnp.where(before, BIG, first[:, window]), axis=1, keepdims=True)
        dprev[128 * c : 128 * c + 128, :] = jnp.broadcast_to(t - start, (128, 128))
        dnext[128 * c : 128 * c + 128, :] = jnp.broadcast_to(stop - t, (128, 128))


def attention_bias(dprev, dnext, bias):
    for i in range(F // 128):
        rows = slice(KOFF + 128 * i, KOFF + 128 * i + 128)
        back = dprev[rows, :].astype(jnp.int32)
        ahead = dnext[rows, :].astype(jnp.int32)
        rem = back & (BLOCK_LEN - 1)
        low = -jnp.minimum(back, rem + LEFT_BLOCKS * BLOCK_LEN)
        high = jnp.minimum(ahead, BLOCK_LEN - rem)
        for half in range(2):
            delta = (
                lax.broadcasted_iota(jnp.int32, (128, 128), 1)
                - lax.broadcasted_iota(jnp.int32, (128, 128), 0)
                + (128 * half - KOFF)
            )
            ok = (delta >= low) & (delta < high)
            bias[i, :, 128 * half : 128 * half + 128] = jnp.where(ok, F32(0.0), F32(-1e30))


def conv_norm(xf, taps, gain, dprev, dnext, hid, nrm, first, last, place_of):
    step = 32
    tiles = D // 128

    def block(n, _):
        r0, d0 = (pl.multiple_of(v, step) for v in place_of(n))
        back = dprev[pl.ds(r0, step), :]
        ahead = dnext[pl.ds(r0, step), :]
        keep = [back >= F32(4 - j) if j < 4 else ahead > F32(j - 4) for j in range(9)]
        hs = []
        total = jnp.zeros((step, 128), F32)
        for c in range(tiles):
            cols = slice(128 * c, 128 * c + 128)
            centre = xf[c, pl.ds(r0 + 16, step), :]
            acc = centre * taps[4:5, cols]
            for j in range(9):
                if j == 4:
                    continue
                term = xf[c, pl.ds(r0 + 12 + j, step), :] * taps[j : j + 1, cols]
                acc = acc + jnp.where(keep[j], term, F32(0.0))
            h16 = (centre + acc).astype(BF16)
            hid[pl.ds(r0, step), cols] = h16
            h = h16.astype(F32)
            hs.append(h)
            total = total + h
        mean = jnp.sum(total, axis=1, keepdims=True) * F32(1.0 / D)
        hs = [h - mean for h in hs]
        square = jnp.zeros((step, 128), F32)
        for h in hs:
            square = square + h * h
        var = jnp.sum(square, axis=1, keepdims=True) * F32(1.0 / D)
        scale = lax.rsqrt(var + F32(1e-5))
        for c in range(tiles):
            cols = slice(128 * c, 128 * c + 128)
            nrm[pl.ds(d0, step), cols] = (hs[c] * scale * gain[:, cols]).astype(BF16)
        return 0

    lax.fori_loop(first, last, block, 0)


def project(nrm, rows, weights, base, out, pieces):
    def tile(n, _):
        cols = pl.ds(pl.multiple_of(n * 256, 256), 256)
        value = jnp.dot(
            nrm[rows, :],
            weights[:, pl.ds(pl.multiple_of(base + n * 256, 256), 256)],
            preferred_element_type=F32,
        ).astype(BF16)
        at = 0
        for place, size in pieces:
            out[place : place + size, cols] = value[at : at + size]
            at += size
        return 0

    lax.fori_loop(0, D // 256, tile, 0)


def attend(heads, tiles, q, k, v, bias, attn):
    factor = 1.4426950408889634 / 128.0**0.5
    work = []
    for h in heads:
        lanes = pl.ds(pl.multiple_of(h * 128, 128), 128)
        for i in tiles:
            own = slice(128 * i, 128 * i + 128)
            seen = slice(128 * i, 128 * i + 256)
            s = lax.dot_general(
                q[own, lanes], k[seen, lanes], (((1,), (1,)), ((), ())), preferred_element_type=F32
            )
            work.append((own, seen, lanes, s + bias[i]))
    tops = [jnp.max(s, axis=1, keepdims=True) for _, _, _, s in work]
    expos = [jnp.exp2((item[3] - top) * factor) for item, top in zip(work, tops)]
    norms = [1.0 / jnp.sum(e, axis=1, keepdims=True) for e in expos]
    for (own, seen, lanes, _), e, norm in zip(work, expos, norms):
        w = (e * norm).astype(BF16)
        attn[own, lanes] = jnp.dot(w, v[seen, lanes], preferred_element_type=F32).astype(BF16)


def placement_of(row):
    rows = row.shape[1]
    square = lax.broadcasted_iota(jnp.int32, (rows, rows), 0) == lax.broadcasted_iota(
        jnp.int32, (rows, rows), 1
    )
    spread = jnp.where(square, row.astype(F32), F32(0.0))
    owner = jnp.sum(spread, axis=1, keepdims=True).astype(jnp.int32)
    lane = lax.broadcasted_iota(jnp.int32, (rows, 128), 1)
    hot = jnp.where(owner == lane, F32(1.0), F32(0.0))
    lower = jnp.where(
        lax.broadcasted_iota(jnp.int32, (rows, rows), 1)
        < lax.broadcasted_iota(jnp.int32, (rows, rows), 0),
        F32(1.0),
        F32(0.0),
    ).astype(BF16)
    before = jnp.dot(lower, hot.astype(BF16), preferred_element_type=F32)
    rank = jnp.sum(hot * before, axis=1, keepdims=True).astype(jnp.int32)
    slot = owner * 4 + rank
    slot_row = jnp.sum(jnp.where(square, slot.astype(F32), F32(0.0)), axis=0, keepdims=True)
    column = lax.broadcasted_iota(jnp.int32, (128, rows), 0)
    return jnp.where(column == slot_row.astype(jnp.int32), F32(1.0), F32(0.0)).astype(BF16)


def remote(src, dst, sends, recvs, index, target):
    return pltpu.make_async_remote_copy(
        src_ref=src,
        dst_ref=dst,
        send_sem=sends.at[index],
        recv_sem=recvs.at[index],
        device_id=target,
        device_id_type=MESH,
    )


def each(count, body):
    def one(k, _):
        body(k)
        return 0

    lax.fori_loop(1, count, one, 0)


def to_slots(value, wide, slots):
    for c in range(D // 128):
        wide[pl.ds(c, 128, stride=8), :] = value[:, 128 * c : 128 * c + 128].astype(F32)
    for o in range(N_SEQ):
        slots[o] = wide[32 * o : 32 * o + 32, :].astype(BF16)


def from_slots(slots, wide):
    for o in range(N_SEQ):
        wide[32 * o : 32 * o + 32, :] = slots[o].astype(F32)
    return [wide[pl.ds(c, 128, stride=8), :].astype(BF16) for c in range(D // 128)]


def whole_kernel(
    frames, begins, owner_hbm, taps_hbm, gain_hbm, wqkv_hbm, wout_hbm, cot_hbm,
    audio, fin,
    xb, xf, bgs, dprev, dnext, hid, nrm, edge, qs, ks, vs, bias, attn, wqkv, wout,
    cg, wide, place, ahl, asp, aall, perm, part, partb, xr, quarter, zr, aout, arecv,
    owner, taps, gain,
    local_sems, halo_s, halo_r, cot_s, cot_r, relay_s, relay_r, a_s, a_r, x_s, x_r, z_s, z_r,
    t_s, t_r, m_s, m_r, h0_s, h0_r, h1_s, h1_r, p0_s, p0_r, p1_s, p1_r, c_s, c_r,
):
    z = lax.axis_index("grp")
    s = lax.axis_index("seq")
    x = s // GROUP
    j = s % GROUP
    y = j // 2
    c = j % 2

    def seq(k):
        return {"seq": (s + k) % N_SEQ}

    def grp(k):
        return {"grp": (z + k) % N_GRP}

    def at_head(kx, n):
        return {"seq": (x + kx) % N_X * GROUP + (j + n) % GROUP}

    def along_x(k):
        return {"seq": (x + k) % N_X * GROUP + j}

    def along_y(k):
        return {"seq": x * GROUP + (y + k) % N_Y * 2 + c}

    other_core = {"seq": x * GROUP + y * 2 + (1 - c)}

    barrier = pltpu.get_barrier_semaphore()

    def greet(target):
        pl.semaphore_signal(barrier, inc=1, device_id=target, device_id_type=MESH)

    each(N_SEQ, lambda k: greet(seq(k)))
    each(N_GRP, lambda k: greet(grp(k)))

    def slots_of(owner_in_row):
        return pl.ds(pl.multiple_of(owner_in_row * 128, 128), 128)

    loads = [
        pltpu.make_async_copy(begins, bgs.at[3], local_sems.at[0]),
        pltpu.make_async_copy(frames.at[0], xb.at[pl.ds(LEFT, F)], local_sems.at[1]),
        pltpu.make_async_copy(taps_hbm, taps, local_sems.at[2]),
        pltpu.make_async_copy(gain_hbm, gain, local_sems.at[3]),
        pltpu.make_async_copy(cot_hbm.at[0], cg.at[slots_of(j)], local_sems.at[4]),
        pltpu.make_async_copy(owner_hbm, owner, local_sems.at[5]),
        pltpu.make_async_copy(wqkv_hbm, wqkv, local_sems.at[6]),
        pltpu.make_async_copy(wout_hbm, wout, local_sems.at[7]),
    ]
    for copy in loads:
        copy.start()
    for copy in loads[:4]:
        copy.wait()
    none = jnp.zeros((1, F), jnp.int32)
    alone = jnp.concatenate([none, none, none, bgs[3], none[:, :128]], axis=1)
    bounds(alone, s * F, F * N_SEQ, dprev, dnext)
    for tile in range(D // 128):
        xf[tile, LEFT : LEFT + F] = xb[LEFT : LEFT + F, 128 * tile : 128 * tile + 128].astype(F32)
    conv_norm(
        xf, taps, gain, dprev, dnext, hid, nrm, 0, 14, lambda n: (128 + 32 * n, 32 * n)
    )
    loads[4].wait()
    loads[5].wait()
    place[...] = placement_of(owner[...])
    loads[6].wait()
    project(nrm, slice(0, 448), wqkv, 0, qs, ((32, 448),))

    pl.semaphore_wait(barrier, N_SEQ - 1 + N_GRP - 1)

    halo = [
        remote(xb.at[pl.ds(F, LEFT)], xb.at[pl.ds(0, LEFT)], halo_s, halo_r, 0, seq(1)),
        remote(xb.at[pl.ds(LEFT, RIGHT)], xb.at[pl.ds(LEFT + F, RIGHT)], halo_s, halo_r, 1, seq(N_SEQ - 1)),
        remote(begins, bgs.at[2], halo_s, halo_r, 2, seq(1)),
        remote(begins, bgs.at[1], halo_s, halo_r, 3, seq(2)),
        remote(begins, bgs.at[0], halo_s, halo_r, 4, seq(3)),
        remote(begins, bgs.at[4], halo_s, halo_r, 5, seq(N_SEQ - 1)),
    ]
    for copy in halo:
        copy.start()

    def copy_cot(k):
        block = cg.at[slots_of(j)]
        return remote(block, block, cot_s, cot_r, k, along_y(k))

    def copy_relay(k):
        block = cg.at[slots_of((y + N_Y - k) % N_Y * 2 + c)]
        return remote(block, block, relay_s, relay_r, k, other_core)

    for k in (1, 3, 2):
        copy_cot(k).start()
    copy_relay(0).start()

    project(nrm, slice(0, 448), wqkv, D, ks, ((128, 448),))
    project(nrm, slice(0, 448), wqkv, 2 * D, vs, ((128, 448),))
    for copy in halo[2:]:
        copy.wait_recv()
    marks = jnp.concatenate([bgs[0], bgs[1], bgs[2], bgs[3], bgs[4][:, :128]], axis=1)
    bounds(marks, s * F, F * N_SEQ, dprev, dnext)
    attention_bias(dprev, dnext, bias)

    def middle(n, _):
        attend((2 * n, 2 * n + 1), (1, 2), qs, ks, vs, bias, attn)
        return 0

    lax.fori_loop(0, HEADS // 2, middle, 0)
    for copy in halo[:2]:
        copy.wait_recv()
    for tile in range(D // 128):
        cols = slice(128 * tile, 128 * tile + 128)
        xf[tile, :LEFT] = xb[:LEFT, cols].astype(F32)
        xf[tile, LEFT + F :] = xb[LEFT + F :, cols].astype(F32)
    conv_norm(
        xf, taps, gain, dprev, dnext, hid, edge, 0, 6,
        lambda n: (32 * n + 448 * (n // 4), 32 * n),
    )
    project(edge, slice(96, 160), wqkv, 0, qs, ((0, 32), (480, 32)))
    project(edge, slice(0, 192), wqkv, D, ks, ((0, 128), (576, 64)))
    project(edge, slice(0, 192), wqkv, 2 * D, vs, ((0, 128), (576, 64)))

    rows = F // SUB
    gather = jnp.where(
        lax.broadcasted_iota(jnp.int32, (rows, F), 1) >> 3
        == lax.broadcasted_iota(jnp.int32, (rows, F), 0),
        F32(1.0),
        F32(0.0),
    ).astype(BF16)

    def copy_a(kx, n):
        block = asp.at[(j + n) % HEADS, (x + kx) % N_X]
        here = pl.ds(pl.multiple_of(s * 32, 32), 32)
        return remote(block, aall.at[here], a_s, a_r, n * N_X + kx, at_head(kx, n))

    def two_heads(n, m):
        pair = ((j + n) % HEADS, (j + m) % HEADS)
        attend(pair, (0, 3), qs, ks, vs, bias, attn)
        for h in pair:
            lanes = pl.ds(pl.multiple_of(h * 128, 128), 128)
            asum = jnp.dot(gather, attn[:, lanes], preferred_element_type=F32)
            high = asum.astype(BF16)
            low = (asum - high.astype(F32)).astype(BF16)
            ahl[0, :, lanes] = high
            ahl[1, :, lanes] = low
            spread = jnp.dot(place[...], high, preferred_element_type=F32)
            spread = spread + jnp.dot(place[...], low, preferred_element_type=F32)
            for part_x in range(N_X):
                asp[h, part_x] = spread[32 * part_x : 32 * part_x + 32]

    def two_heads_and_send(p, _):
        two_heads(2 * p + 1, 2 * p + 2)
        for n in (2 * p + 1, 2 * p + 2):
            for kx in range(N_X):
                copy_a(kx, n).start()
        return 0

    lax.fori_loop(0, 3, two_heads_and_send, 0)
    two_heads(7, 0)
    for kx in range(1, N_X):
        copy_a(kx, 0).start()
    for kx in range(N_X):
        copy_a(kx, 7).start()
    aall[pl.ds(pl.multiple_of(s * 32, 32), 32), :] = asp[j, x]
    for k in (1, 3, 2):
        copy_cot(k).wait_recv()
        copy_relay(k).start()

    loads[7].wait()
    hsum = jnp.dot(gather, hid[KOFF : KOFF + F, :], preferred_element_type=F32)
    proj = jnp.dot(ahl[0], wout[...], preferred_element_type=F32)
    proj = proj + jnp.dot(ahl[1], wout[...], preferred_element_type=F32)
    pooled = ((hsum + proj) * F32(1.0 / SUB)).astype(BF16)
    dims = (((0,), (0,)), ((), ()))
    outgoing = jnp.dot(place[...], pooled, preferred_element_type=F32)
    to_slots(outgoing, wide, aout)

    def copy_audio(k):
        return remote(aout.at[(s + k) % N_SEQ], arecv.at[s], m_s, m_r, k, seq(k))

    each(N_SEQ, lambda k: copy_audio(k).start())
    arecv[s] = aout[s]

    for k in range(N_Y):
        copy_relay(k).wait_recv()

    def got_a(n, _):
        for kx in range(N_X):
            copy_a(kx, n).wait_recv()
        return 0

    for kx in range(1, N_X):
        copy_a(kx, 0).wait_recv()
    lax.fori_loop(1, HEADS, got_a, 0)
    for m in range(GROUP):
        for rank in range(4):
            perm[pl.ds(m * 128 + rank, N_SEQ, stride=4), :] = aall[
                pl.ds(m * 4 + rank, N_SEQ, stride=32), :
            ]
    apart = perm[...]
    ahigh = apart.astype(BF16)
    alow = (apart - ahigh.astype(F32)).astype(BF16)
    part[...] = lax.dot_general(ahigh, cg[...], dims, preferred_element_type=F32)
    part[...] += lax.dot_general(alow, cg[...], dims, preferred_element_type=F32)
    partb[...] = part[...].astype(BF16)

    def rows_of(place_x):
        return pl.ds(pl.multiple_of(place_x * 32, 32), 32)

    def copy_x(k):
        return remote(partb.at[rows_of((x + k) % N_X)], xr.at[k], x_s, x_r, k, along_x(k))

    for k in range(1, N_X):
        copy_x(k).start()
    for k in range(1, N_X):
        copy_x(k).wait_recv()
    total = part[rows_of(x), :]
    for k in range(1, N_X):
        total = total + xr[k].astype(F32)
    for tile in range(N_GRP):
        quarter[tile] = total[:, 128 * tile : 128 * tile + 128]

    def copy_z(k):
        return remote(quarter.at[(z + k) % N_GRP], zr.at[k], z_s, z_r, k, grp(k))

    for k in range(1, N_GRP):
        copy_z(k).start()
    for k in range(1, N_GRP):
        copy_z(k).wait_recv()
    tile_sum = quarter[z]
    for k in range(1, N_GRP):
        tile_sum = tile_sum + zr[k]
    own_cols = pl.ds(pl.multiple_of(z * 128, 128), 128)
    fin[y, c, x, :, own_cols] = (tile_sum * F32(1.0 / (128 * SUB))).astype(BF16)

    def copy_t(k):
        tile = fin.at[y, c, x, :, own_cols]
        return remote(tile, tile, t_s, t_r, k, grp(k))

    for k in range(1, N_GRP):
        copy_t(k).start()
    for k in range(1, N_GRP):
        copy_t(k).wait_recv()

    first, second = pl.ds(0, D // 2), pl.ds(D // 2, D // 2)

    def copy_h0(k):
        block = fin.at[y, c, x, :, first]
        return remote(block, block, h0_s, h0_r, k, along_x(k))

    def copy_h1(k):
        block = fin.at[y, c, x, :, second]
        return remote(block, block, h1_s, h1_r, k, along_y(k))

    def copy_p0(kx, ky):
        block = fin.at[y, c, (x + N_X - kx) % N_X, :, first]
        return remote(block, block, p0_s, p0_r, kx * N_Y + ky, along_y(ky))

    def copy_p1(ky, kx):
        block = fin.at[(y + N_Y - ky) % N_Y, c, x, :, second]
        return remote(block, block, p1_s, p1_r, ky * N_X + kx, along_x(kx))

    def copy_c0(k):
        block = fin.at[(y + N_Y - k) % N_Y, c, :, :, first]
        return remote(block, block, c_s, c_r, k, other_core)

    def copy_c1(k):
        block = fin.at[:, c, (x + N_X - k) % N_X, :, second]
        return remote(block, block, c_s, c_r, N_Y + k, other_core)

    for k in (1, 3, 2):
        copy_h0(k).start()
        copy_h1(k).start()
    for k in (1, 3, 2):
        copy_p0(0, k).start()
        copy_p1(0, k).start()
    for k in (1, 3, 2):
        copy_h0(k).wait_recv()
        for ky in (1, 3, 2):
            copy_p0(k, ky).start()
        copy_h1(k).wait_recv()
        for kx in (1, 3, 2):
            copy_p1(k, kx).start()
    copy_c0(0).start()
    copy_c1(0).start()

    def got_audio(k):
        source = (s + N_SEQ - k) % N_SEQ
        remote(arecv.at[source], arecv.at[source], m_s, m_r, k, seq(k)).wait_recv()

    each(N_SEQ, got_audio)
    for tile, value in enumerate(from_slots(arecv, wide)):
        audio[:, 128 * tile : 128 * tile + 128] = value

    for k in (1, 3, 2):
        for other in range(N_X):
            copy_p0(other, k).wait_recv()
        copy_c0(k).start()
        for other in range(N_Y):
            copy_p1(other, k).wait_recv()
        copy_c1(k).start()
    for k in range(N_Y):
        copy_c0(k).wait_recv()
        copy_c1(k).wait_recv()

    for copy in halo:
        copy.wait_send()

    each(N_SEQ, lambda k: copy_audio(k).wait_send())

    def sent_a(n, _):
        for kx in range(N_X):
            copy_a(kx, n).wait_send()
        return 0

    for kx in range(1, N_X):
        copy_a(kx, 0).wait_send()
    lax.fori_loop(1, HEADS, sent_a, 0)

    def sent_z(k):
        copy_z(k).wait_send()
        copy_t(k).wait_send()

    each(N_GRP, sent_z)
    for k in range(1, N_X):
        copy_cot(k).wait_send()
        copy_x(k).wait_send()
        copy_h0(k).wait_send()
        copy_h1(k).wait_send()
    for k in range(N_Y):
        copy_relay(k).wait_send()
        copy_c0(k).wait_send()
        copy_c1(k).wait_send()
        for other in range(1, N_X):
            copy_p0(k, other).wait_send()
            copy_p1(k, other).wait_send()


def shards(frames, begins, owner, conv_kernel, norm_gain, w_qkv, w_out, cotangent):
    vm = pl.BlockSpec(memory_space=pltpu.VMEM)
    hbm = pl.BlockSpec(memory_space=pltpu.HBM)
    dma = pltpu.SemaphoreType.DMA
    audio, grad = pl.pallas_call(
        whole_kernel,
        out_shape=(
            jax.ShapeDtypeStruct((128, D), BF16),
            jax.ShapeDtypeStruct((N_Y, 2, N_X, 32, D), BF16),
        ),
        in_specs=[hbm] * 8,
        out_specs=(vm, vm),
        scratch_shapes=[
            pltpu.VMEM((LEFT + F + RIGHT, D), BF16),
            pltpu.VMEM((8, LEFT + F + RIGHT, 128), F32),
            pltpu.VMEM((5, 1, F), jnp.int32),
            pltpu.VMEM((KV, 128), F32),
            pltpu.VMEM((KV, 128), F32),
            pltpu.VMEM((KV, D), BF16),
            pltpu.VMEM((448, D), BF16),
            pltpu.VMEM((192, D), BF16),
            pltpu.VMEM((F, D), BF16),
            pltpu.VMEM((KV, D), BF16),
            pltpu.VMEM((KV, D), BF16),
            pltpu.VMEM((4, 128, 256), F32),
            pltpu.VMEM((F, D), BF16),
            pltpu.VMEM((D, 3 * D), BF16),
            pltpu.VMEM((D, D), BF16),
            pltpu.VMEM((GROUP * 128, D), BF16),
            pltpu.VMEM((1024, 128), F32),
            pltpu.VMEM((128, 64), BF16),
            pltpu.VMEM((2, 64, D), BF16),
            pltpu.VMEM((HEADS, N_X, 32, 128), F32),
            pltpu.VMEM((1024, 128), F32),
            pltpu.VMEM((1024, 128), F32),
            pltpu.VMEM((128, D), F32),
            pltpu.VMEM((128, D), BF16),
            pltpu.VMEM((N_X, 32, D), BF16),
            pltpu.VMEM((N_GRP, 32, 128), F32),
            pltpu.VMEM((N_GRP, 32, 128), F32),
            pltpu.VMEM((N_SEQ, 32, 128), BF16),
            pltpu.VMEM((N_SEQ, 32, 128), BF16),
            pltpu.VMEM((1, 64), jnp.int32),
            pltpu.VMEM((9, D), F32),
            pltpu.VMEM((1, D), F32),
            dma((8,)),
            dma((6,)), dma((6,)),
            dma((N_Y,)), dma((N_Y,)),
            dma((N_Y,)), dma((N_Y,)),
            dma((N_SEQ,)), dma((N_SEQ,)),
            dma((N_X,)), dma((N_X,)),
            dma((N_GRP,)), dma((N_GRP,)),
            dma((N_GRP,)), dma((N_GRP,)),
            dma((N_SEQ,)), dma((N_SEQ,)),
            dma((N_X,)), dma((N_X,)),
            dma((N_Y,)), dma((N_Y,)),
            dma((N_X * N_Y,)), dma((N_X * N_Y,)),
            dma((N_X * N_Y,)), dma((N_X * N_Y,)),
            dma((2 * N_Y,)), dma((2 * N_Y,)),
        ],
        compiler_params=pltpu.CompilerParams(
            vmem_limit_bytes=48 * 1024 * 1024, collective_id=0, has_side_effects=True
        ),
        name="whole",
    )(
        *(
            pltpu.with_memory_space_constraint(value, pltpu.HBM)
            for value in (
                frames,
                begins,
                owner.reshape(1, 64),
                conv_kernel,
                norm_gain.reshape(1, D),
                w_qkv,
                w_out,
                cotangent,
            )
        )
    )
    return audio.reshape(1, 128, D), grad.reshape(D, D)


def solution(mesh):
    return jax.shard_map(
        shards,
        mesh=mesh,
        in_specs=(
            P("grp", "seq", None),
            P("grp", "seq"),
            P("grp", "seq", None),
            P(),
            P(),
            P(),
            P(),
            P("grp", "seq", None),
        ),
        out_specs=(P("grp", "seq", None), P()),
        check_vma=False,
    )
```

time: 91.9 us -> 74.8 us (0.81)
  Pallas kernels: 82.1 us -> 72.1 us
  local copies, waits for them, and re-layouts: 8.85 us -> 2.02 us
    pallas_call x1, Pallas kernels: 82.1 us -> 72.1 us  [shards(): pl.pallas_call(whole_kernel, out_shape=(jax.ShapeDtypeStruct((128, D), BF...]
    unnamed x13 -> x2, local copies, waits for them, and re-layouts: 7.29 us -> 2.02 us
where the time goes in v3:
time: 74.8 us
  Pallas kernels  72.1 us (96%)
  local copies, waits for them, and re-layouts  2.02 us (3%)
    pallas_call x1, Pallas kernels, shards(): pl.pallas_call(whole_kernel, out_shape=(jax.ShapeDtypeStruct((128, D), BF...  72.1 us
    unnamed x2, local copies, waits for them, and re-layouts  2.02 us

profile of v3, /device:TPU:1, one launch (start us, length us, event | category | flops | bytes accessed | tf_op | source)
XLA Modules:
  0.0 74.8 jit_solution(11357654515755930126)
XLA Ops:
  0.6 72.1 %whole.1 = (bf16[128,1024]{1,0:T(8,128)(2,1)S(1)}, bf16[4,2,4,32,1024]{4,3,2,1,0:T(8,128)(2,1)S(1)}) custom-call(bf16[1,512,1024]{2,1,0:T(8,128)(2,1)} %frames.1, s32[1,512]{1,0:T(1,128)} %begins.1, s32[1,64]{1,0:T(1,128)} %bitcast.7, f32[9,1024]{1,0:T(8,128)} %taps_hbm.1, f32[1,1024]{1,0:T(1,128)} %bitcast.6, bf16[1024,3072]{1,0:T(8,128)(2,1)} %wqkv_hbm.1, ...), custom_call_target="tpu_custom_call" | custom-call | tf_op jit(solution)/shard_map/whole/pallas_call | solution.py:544
  72.7 0.7 copy.12
  73.4 1.3 %copy.13 = bf16[1024,1024]{1,0:T(8,128)(2,1)} copy(bf16[1024,1024]{1,0:T(8,128)(2,1)S(1)} %bitcast.4) | data formatting | bytes 4194304

commit v4 on v3

--- a/solution.py
+++ b/solution.py
@@ -106,20 +106,13 @@
 
 
 def project(nrm, rows, weights, base, out, pieces):
-    def tile(n, _):
-        cols = pl.ds(pl.multiple_of(n * 256, 256), 256)
-        value = jnp.dot(
-            nrm[rows, :],
-            weights[:, pl.ds(pl.multiple_of(base + n * 256, 256), 256)],
-            preferred_element_type=F32,
-        ).astype(BF16)
-        at = 0
-        for place, size in pieces:
-            out[place : place + size, cols] = value[at : at + size]
-            at += size
-        return 0
-
-    lax.fori_loop(0, D // 256, tile, 0)
+    value = jnp.dot(
+        nrm[rows, :], weights[:, base : base + D], preferred_element_type=F32
+    ).astype(BF16)
+    at = 0
+    for place, size in pieces:
+        out[place : place + size, :] = value[at : at + size]
+        at += size
 
 
 def attend(heads, tiles, q, k, v, bias, attn):
@@ -162,7 +155,9 @@
     slot = owner * 4 + rank
     slot_row = jnp.sum(jnp.where(square, slot.astype(F32), F32(0.0)), axis=0, keepdims=True)
     column = lax.broadcasted_iota(jnp.int32, (128, rows), 0)
-    return jnp.where(column == slot_row.astype(jnp.int32), F32(1.0), F32(0.0)).astype(BF16)
+    by_slot = jnp.where(column == slot_row.astype(jnp.int32), F32(1.0), F32(0.0)).astype(BF16)
+    by_row = jnp.where(lane == slot, F32(1.0), F32(0.0)).astype(BF16)
+    return by_slot, by_row
 
 
 def remote(src, dst, sends, recvs, index, target):
@@ -201,9 +196,9 @@
     frames, begins, owner_hbm, taps_hbm, gain_hbm, wqkv_hbm, wout_hbm, cot_hbm,
     audio, fin,
     xb, xf, bgs, dprev, dnext, hid, nrm, edge, qs, ks, vs, bias, attn, wqkv, wout,
-    cg, wide, place, ahl, asp, aall, perm, part, partb, xr, quarter, zr, aout, arecv,
+    cotv, cots, back, gall, wide, place, pick, ahl, asp, aall, part, tiles, got, aout, arecv,
     owner, taps, gain,
-    local_sems, halo_s, halo_r, cot_s, cot_r, relay_s, relay_r, a_s, a_r, x_s, x_r, z_s, z_r,
+    local_sems, halo_s, halo_r, cot_s, cot_r, g_s, g_r, relay_s, relay_r, a_s, a_r, xz_s, xz_r,
     t_s, t_r, m_s, m_r, h0_s, h0_r, h1_s, h1_r, p0_s, p0_r, p1_s, p1_r, c_s, c_r,
 ):
     z = lax.axis_index("grp")
@@ -219,8 +214,8 @@
     def grp(k):
         return {"grp": (z + k) % N_GRP}
 
-    def at_head(kx, n):
-        return {"seq": (x + kx) % N_X * GROUP + (j + n) % GROUP}
+    def in_group(k):
+        return {"seq": x * GROUP + (j + k) % GROUP}
 
     def along_x(k):
         return {"seq": (x + k) % N_X * GROUP + j}
@@ -235,24 +230,54 @@
     def greet(target):
         pl.semaphore_signal(barrier, inc=1, device_id=target, device_id_type=MESH)
 
+    def across(k):
+        return {"grp": (z + k % N_GRP) % N_GRP, "seq": (x + k // N_GRP) % N_X * GROUP + j}
+
     each(N_SEQ, lambda k: greet(seq(k)))
-    each(N_GRP, lambda k: greet(grp(k)))
-
-    def slots_of(owner_in_row):
-        return pl.ds(pl.multiple_of(owner_in_row * 128, 128), 128)
+
+    def greet_planes(kz):
+        for kx in range(N_X):
+            greet(across(kx * N_GRP + kz))
+
+    each(N_GRP, greet_planes)
+
+    def rows_of(source):
+        return pl.ds(pl.multiple_of(source * 64, 64), 64)
 
     loads = [
         pltpu.make_async_copy(begins, bgs.at[3], local_sems.at[0]),
         pltpu.make_async_copy(frames.at[0], xb.at[pl.ds(LEFT, F)], local_sems.at[1]),
         pltpu.make_async_copy(taps_hbm, taps, local_sems.at[2]),
         pltpu.make_async_copy(gain_hbm, gain, local_sems.at[3]),
-        pltpu.make_async_copy(cot_hbm.at[0], cg.at[slots_of(j)], local_sems.at[4]),
+        pltpu.make_async_copy(cot_hbm.at[0], cotv, local_sems.at[4]),
         pltpu.make_async_copy(owner_hbm, owner, local_sems.at[5]),
         pltpu.make_async_copy(wqkv_hbm, wqkv, local_sems.at[6]),
         pltpu.make_async_copy(wout_hbm, wout, local_sems.at[7]),
     ]
     for copy in loads:
         copy.start()
+    pl.semaphore_wait(barrier, N_SEQ - 1 + N_X * (N_GRP - 1))
+
+    halo = [
+        remote(frames.at[0, pl.ds(F - LEFT, LEFT)], xb.at[pl.ds(0, LEFT)], halo_s, halo_r, 0, seq(1)),
+        remote(frames.at[0, pl.ds(0, RIGHT)], xb.at[pl.ds(LEFT + F, RIGHT)], halo_s, halo_r, 1, seq(N_SEQ - 1)),
+        remote(begins, bgs.at[2], halo_s, halo_r, 2, seq(1)),
+        remote(begins, bgs.at[1], halo_s, halo_r, 3, seq(2)),
+        remote(begins, bgs.at[0], halo_s, halo_r, 4, seq(3)),
+        remote(begins, bgs.at[4], halo_s, halo_r, 5, seq(N_SEQ - 1)),
+    ]
+    for copy in halo[2:] + halo[:2]:
+        copy.start()
+
+    loads[4].wait()
+    to_slots(cotv[...], wide, cots)
+
+    def copy_cot(k):
+        return remote(cots.at[(s + k) % N_SEQ], back.at[s], cot_s, cot_r, k, seq(k))
+
+    each(N_SEQ, lambda k: copy_cot(k).start())
+    back[s] = cots[s]
+
     for copy in loads[:4]:
         copy.wait()
     none = jnp.zeros((1, F), jnp.int32)
@@ -263,36 +288,10 @@
     conv_norm(
         xf, taps, gain, dprev, dnext, hid, nrm, 0, 14, lambda n: (128 + 32 * n, 32 * n)
     )
-    loads[4].wait()
     loads[5].wait()
-    place[...] = placement_of(owner[...])
+    place[...], pick[...] = placement_of(owner[...])
     loads[6].wait()
     project(nrm, slice(0, 448), wqkv, 0, qs, ((32, 448),))
-
-    pl.semaphore_wait(barrier, N_SEQ - 1 + N_GRP - 1)
-
-    halo = [
-        remote(xb.at[pl.ds(F, LEFT)], xb.at[pl.ds(0, LEFT)], halo_s, halo_r, 0, seq(1)),
-        remote(xb.at[pl.ds(LEFT, RIGHT)], xb.at[pl.ds(LEFT + F, RIGHT)], halo_s, halo_r, 1, seq(N_SEQ - 1)),
-        remote(begins, bgs.at[2], halo_s, halo_r, 2, seq(1)),
-        remote(begins, bgs.at[1], halo_s, halo_r, 3, seq(2)),
-        remote(begins, bgs.at[0], halo_s, halo_r, 4, seq(3)),
-        remote(begins, bgs.at[4], halo_s, halo_r, 5, seq(N_SEQ - 1)),
-    ]
-    for copy in halo:
-        copy.start()
-
-    def copy_cot(k):
-        block = cg.at[slots_of(j)]
-        return remote(block, block, cot_s, cot_r, k, along_y(k))
-
-    def copy_relay(k):
-        block = cg.at[slots_of((y + N_Y - k) % N_Y * 2 + c)]
-        return remote(block, block, relay_s, relay_r, k, other_core)
-
-    for k in (1, 3, 2):
-        copy_cot(k).start()
-    copy_relay(0).start()
 
     project(nrm, slice(0, 448), wqkv, D, ks, ((128, 448),))
     project(nrm, slice(0, 448), wqkv, 2 * D, vs, ((128, 448),))
@@ -307,6 +306,28 @@
         return 0
 
     lax.fori_loop(0, HEADS // 2, middle, 0)
+
+    def got_cot(k):
+        source = (s + N_SEQ - k) % N_SEQ
+        remote(back.at[source], back.at[source], cot_s, cot_r, k, seq(k)).wait_recv()
+
+    each(N_SEQ, got_cot)
+    for tile, value in enumerate(from_slots(back, wide)):
+        gall[rows_of(j), 128 * tile : 128 * tile + 128] = jnp.dot(
+            pick[...], value, preferred_element_type=F32
+        ).astype(BF16)
+
+    def copy_g(k):
+        block = gall.at[rows_of(j)]
+        return remote(block, block, g_s, g_r, k, along_y(k))
+
+    def copy_relay(k):
+        block = gall.at[rows_of((y + N_Y - k) % N_Y * 2 + c)]
+        return remote(block, block, relay_s, relay_r, k, other_core)
+
+    for k in (1, 3, 2):
+        copy_g(k).start()
+    copy_relay(0).start()
     for copy in halo[:2]:
         copy.wait_recv()
     for tile in range(D // 128):
@@ -329,10 +350,8 @@
         F32(0.0),
     ).astype(BF16)
 
-    def copy_a(kx, n):
-        block = asp.at[(j + n) % HEADS, (x + kx) % N_X]
-        here = pl.ds(pl.multiple_of(s * 32, 32), 32)
-        return remote(block, aall.at[here], a_s, a_r, n * N_X + kx, at_head(kx, n))
+    def copy_a(n):
+        return remote(asp.at[(j + n) % HEADS], aall.at[:, rows_of(j)], a_s, a_r, n, in_group(n))
 
     def two_heads(n, m):
         pair = ((j + n) % HEADS, (j + m) % HEADS)
@@ -344,27 +363,21 @@
             low = (asum - high.astype(F32)).astype(BF16)
             ahl[0, :, lanes] = high
             ahl[1, :, lanes] = low
-            spread = jnp.dot(place[...], high, preferred_element_type=F32)
-            spread = spread + jnp.dot(place[...], low, preferred_element_type=F32)
-            for part_x in range(N_X):
-                asp[h, part_x] = spread[32 * part_x : 32 * part_x + 32]
+            asp[h, 0] = high
+            asp[h, 1] = low
 
     def two_heads_and_send(p, _):
         two_heads(2 * p + 1, 2 * p + 2)
-        for n in (2 * p + 1, 2 * p + 2):
-            for kx in range(N_X):
-                copy_a(kx, n).start()
+        copy_a(2 * p + 1).start()
+        copy_a(2 * p + 2).start()
         return 0
 
     lax.fori_loop(0, 3, two_heads_and_send, 0)
     two_heads(7, 0)
-    for kx in range(1, N_X):
-        copy_a(kx, 0).start()
-    for kx in range(N_X):
-        copy_a(kx, 7).start()
-    aall[pl.ds(pl.multiple_of(s * 32, 32), 32), :] = asp[j, x]
+    copy_a(7).start()
+    aall[:, rows_of(j), :] = asp[j]
     for k in (1, 3, 2):
-        copy_cot(k).wait_recv()
+        copy_g(k).wait_recv()
         copy_relay(k).start()
 
     loads[7].wait()
@@ -385,52 +398,24 @@
     for k in range(N_Y):
         copy_relay(k).wait_recv()
 
-    def got_a(n, _):
-        for kx in range(N_X):
-            copy_a(kx, n).wait_recv()
-        return 0
-
-    for kx in range(1, N_X):
-        copy_a(kx, 0).wait_recv()
-    lax.fori_loop(1, HEADS, got_a, 0)
-    for m in range(GROUP):
-        for rank in range(4):
-            perm[pl.ds(m * 128 + rank, N_SEQ, stride=4), :] = aall[
-                pl.ds(m * 4 + rank, N_SEQ, stride=32), :
-            ]
-    apart = perm[...]
-    ahigh = apart.astype(BF16)
-    alow = (apart - ahigh.astype(F32)).astype(BF16)
-    part[...] = lax.dot_general(ahigh, cg[...], dims, preferred_element_type=F32)
-    part[...] += lax.dot_general(alow, cg[...], dims, preferred_element_type=F32)
-    partb[...] = part[...].astype(BF16)
-
-    def rows_of(place_x):
-        return pl.ds(pl.multiple_of(place_x * 32, 32), 32)
-
-    def copy_x(k):
-        return remote(partb.at[rows_of((x + k) % N_X)], xr.at[k], x_s, x_r, k, along_x(k))
-
-    for k in range(1, N_X):
-        copy_x(k).start()
-    for k in range(1, N_X):
-        copy_x(k).wait_recv()
-    total = part[rows_of(x), :]
-    for k in range(1, N_X):
-        total = total + xr[k].astype(F32)
-    for tile in range(N_GRP):
-        quarter[tile] = total[:, 128 * tile : 128 * tile + 128]
-
-    def copy_z(k):
-        return remote(quarter.at[(z + k) % N_GRP], zr.at[k], z_s, z_r, k, grp(k))
-
-    for k in range(1, N_GRP):
-        copy_z(k).start()
-    for k in range(1, N_GRP):
-        copy_z(k).wait_recv()
-    tile_sum = quarter[z]
-    for k in range(1, N_GRP):
-        tile_sum = tile_sum + zr[k]
+    each(GROUP, lambda k: copy_a(k).wait_recv())
+    part[...] = lax.dot_general(aall[0], gall[...], dims, preferred_element_type=F32)
+    part[...] += lax.dot_general(aall[1], gall[...], dims, preferred_element_type=F32)
+    for px in range(N_X):
+        for pz in range(N_GRP):
+            tiles[px, pz] = part[32 * px : 32 * px + 32, 128 * pz : 128 * pz + 128].astype(BF16)
+
+    def copy_xz(k):
+        block = tiles.at[(x + k // N_GRP) % N_X, (z + k % N_GRP) % N_GRP]
+        return remote(block, got.at[k], xz_s, xz_r, k, across(k))
+
+    each(N_X * N_GRP, lambda k: copy_xz(k).start())
+    tile_sum = part[
+        pl.ds(pl.multiple_of(x * 32, 32), 32), pl.ds(pl.multiple_of(z * 128, 128), 128)
+    ]
+    each(N_X * N_GRP, lambda k: copy_xz(k).wait_recv())
+    for k in range(1, N_X * N_GRP):
+        tile_sum = tile_sum + got[k].astype(F32)
     own_cols = pl.ds(pl.multiple_of(z * 128, 128), 128)
     fin[y, c, x, :, own_cols] = (tile_sum * F32(1.0 / (128 * SUB))).astype(BF16)
 
@@ -509,23 +494,12 @@
 
     each(N_SEQ, lambda k: copy_audio(k).wait_send())
 
-    def sent_a(n, _):
-        for kx in range(N_X):
-            copy_a(kx, n).wait_send()
-        return 0
-
-    for kx in range(1, N_X):
-        copy_a(kx, 0).wait_send()
-    lax.fori_loop(1, HEADS, sent_a, 0)
-
-    def sent_z(k):
-        copy_z(k).wait_send()
-        copy_t(k).wait_send()
-
-    each(N_GRP, sent_z)
+    each(N_SEQ, lambda k: copy_cot(k).wait_send())
+    each(GROUP, lambda k: copy_a(k).wait_send())
+    each(N_X * N_GRP, lambda k: copy_xz(k).wait_send())
+    each(N_GRP, lambda k: copy_t(k).wait_send())
     for k in range(1, N_X):
-        copy_cot(k).wait_send()
-        copy_x(k).wait_send()
+        copy_g(k).wait_send()
         copy_h0(k).wait_send()
         copy_h1(k).wait_send()
     for k in range(N_Y):
@@ -565,18 +539,19 @@
             pltpu.VMEM((F, D), BF16),
             pltpu.VMEM((D, 3 * D), BF16),
             pltpu.VMEM((D, D), BF16),
-            pltpu.VMEM((GROUP * 128, D), BF16),
+            pltpu.VMEM((128, D), BF16),
+            pltpu.VMEM((N_SEQ, 32, 128), BF16),
+            pltpu.VMEM((N_SEQ, 32, 128), BF16),
+            pltpu.VMEM((GROUP * 64, D), BF16),
             pltpu.VMEM((1024, 128), F32),
             pltpu.VMEM((128, 64), BF16),
+            pltpu.VMEM((64, 128), BF16),
             pltpu.VMEM((2, 64, D), BF16),
-            pltpu.VMEM((HEADS, N_X, 32, 128), F32),
-            pltpu.VMEM((1024, 128), F32),
-            pltpu.VMEM((1024, 128), F32),
+            pltpu.VMEM((HEADS, 2, 64, 128), BF16),
+            pltpu.VMEM((2, GROUP * 64, 128), BF16),
             pltpu.VMEM((128, D), F32),
-            pltpu.VMEM((128, D), BF16),
-            pltpu.VMEM((N_X, 32, D), BF16),
-            pltpu.VMEM((N_GRP, 32, 128), F32),
-            pltpu.VMEM((N_GRP, 32, 128), F32),
+            pltpu.VMEM((N_X, N_GRP, 32, 128), BF16),
+            pltpu.VMEM((N_X * N_GRP, 32, 128), BF16),
             pltpu.VMEM((N_SEQ, 32, 128), BF16),
             pltpu.VMEM((N_SEQ, 32, 128), BF16),
             pltpu.VMEM((1, 64), jnp.int32),
@@ -584,11 +559,11 @@
             pltpu.VMEM((1, D), F32),
             dma((8,)),
             dma((6,)), dma((6,)),
+            dma((N_SEQ,)), dma((N_SEQ,)),
             dma((N_Y,)), dma((N_Y,)),
             dma((N_Y,)), dma((N_Y,)),
-            dma((N_SEQ,)), dma((N_SEQ,)),
-            dma((N_X,)), dma((N_X,)),
-            dma((N_GRP,)), dma((N_GRP,)),
+            dma((GROUP,)), dma((GROUP,)),
+            dma((N_X * N_GRP,)), dma((N_X * N_GRP,)),
             dma((N_GRP,)), dma((N_GRP,)),
             dma((N_SEQ,)), dma((N_SEQ,)),
             dma((N_X,)), dma((N_X,)),

time: 74.8 us -> 69.8 us (0.933)
  Pallas kernels: 72.1 us -> 67.1 us
    pallas_call x1, Pallas kernels: 72.1 us -> 67.1 us  [shards(): pl.pallas_call(whole_kernel, out_shape=(jax.ShapeDtypeStruct((128, D), BF...]
where the time goes in v4:
time: 69.8 us
  Pallas kernels  67.1 us (96%)
  local copies, waits for them, and re-layouts  2.02 us (3%)
    pallas_call x1, Pallas kernels, shards(): pl.pallas_call(whole_kernel, out_shape=(jax.ShapeDtypeStruct((128, D), BF...  67.1 us
    unnamed x2, local copies, waits for them, and re-layouts  2.02 us

profile of v4, /device:TPU:1, one launch (start us, length us, event | category | flops | bytes accessed | tf_op | source)
XLA Modules:
  0.0 69.8 jit_solution(13965339880233045168)
XLA Ops:
  0.6 67.1 %whole.1 = (bf16[128,1024]{1,0:T(8,128)(2,1)S(1)}, bf16[4,2,4,32,1024]{4,3,2,1,0:T(8,128)(2,1)S(1)}) custom-call(bf16[1,512,1024]{2,1,0:T(8,128)(2,1)} %frames.1, s32[1,512]{1,0:T(1,128)} %begins.1, s32[1,64]{1,0:T(1,128)} %bitcast.7, f32[9,1024]{1,0:T(8,128)} %taps_hbm.1, f32[1,1024]{1,0:T(1,128)} %bitcast.6, bf16[1024,3072]{1,0:T(8,128)(2,1)} %wqkv_hbm.1, ...), custom_call_target="tpu_custom_call" | custom-call | tf_op jit(solution)/shard_map/whole/pallas_call | solution.py:518
  67.7 0.7 %copy.12 = bf16[1,128,1024]{2,1,0:T(8,128)(2,1)} copy(bf16[1,128,1024]{2,1,0:T(8,128)(2,1)S(1)} %bitcast.5) | data formatting | bytes 524288
  68.4 1.3 %copy.13 = bf16[1024,1024]{1,0:T(8,128)(2,1)} copy(bf16[1024,1024]{1,0:T(8,128)(2,1)S(1)} %bitcast.4) | data formatting | bytes 4194304

commit v5 on v4

--- a/solution.py
+++ b/solution.py
@@ -66,7 +66,7 @@
 
 
 def conv_norm(xf, taps, gain, dprev, dnext, hid, nrm, first, last, place_of):
-    step = 32
+    step = 64
     tiles = D // 128
 
     def block(n, _):
@@ -256,6 +256,17 @@
     ]
     for copy in loads:
         copy.start()
+    for copy in loads[:4]:
+        copy.wait()
+    none = jnp.zeros((1, F), jnp.int32)
+    alone = jnp.concatenate([none, none, none, bgs[3], none[:, :128]], axis=1)
+    bounds(alone, s * F, F * N_SEQ, dprev, dnext)
+    for tile in range(D // 128):
+        xf[tile, LEFT : LEFT + F] = xb[LEFT : LEFT + F, 128 * tile : 128 * tile + 128].astype(F32)
+    loads[4].wait()
+    to_slots(cotv[...], wide, cots)
+    inner = lambda n: (128 + 64 * n, 64 * n)
+    conv_norm(xf, taps, gain, dprev, dnext, hid, nrm, 0, 4, inner)
     pl.semaphore_wait(barrier, N_SEQ - 1 + N_X * (N_GRP - 1))
 
     halo = [
@@ -266,28 +277,18 @@
         remote(begins, bgs.at[0], halo_s, halo_r, 4, seq(3)),
         remote(begins, bgs.at[4], halo_s, halo_r, 5, seq(N_SEQ - 1)),
     ]
-    for copy in halo[2:] + halo[:2]:
+    for copy in halo[2:]:
         copy.start()
-
-    loads[4].wait()
-    to_slots(cotv[...], wide, cots)
 
     def copy_cot(k):
         return remote(cots.at[(s + k) % N_SEQ], back.at[s], cot_s, cot_r, k, seq(k))
 
     each(N_SEQ, lambda k: copy_cot(k).start())
+    for copy in halo[:2]:
+        copy.start()
     back[s] = cots[s]
 
-    for copy in loads[:4]:
-        copy.wait()
-    none = jnp.zeros((1, F), jnp.int32)
-    alone = jnp.concatenate([none, none, none, bgs[3], none[:, :128]], axis=1)
-    bounds(alone, s * F, F * N_SEQ, dprev, dnext)
-    for tile in range(D // 128):
-        xf[tile, LEFT : LEFT + F] = xb[LEFT : LEFT + F, 128 * tile : 128 * tile + 128].astype(F32)
-    conv_norm(
-        xf, taps, gain, dprev, dnext, hid, nrm, 0, 14, lambda n: (128 + 32 * n, 32 * n)
-    )
+    conv_norm(xf, taps, gain, dprev, dnext, hid, nrm, 4, 7, inner)
     loads[5].wait()
     place[...], pick[...] = placement_of(owner[...])
     loads[6].wait()
@@ -301,12 +302,6 @@
     bounds(marks, s * F, F * N_SEQ, dprev, dnext)
     attention_bias(dprev, dnext, bias)
 
-    def middle(n, _):
-        attend((2 * n, 2 * n + 1), (1, 2), qs, ks, vs, bias, attn)
-        return 0
-
-    lax.fori_loop(0, HEADS // 2, middle, 0)
-
     def got_cot(k):
         source = (s + N_SEQ - k) % N_SEQ
         remote(back.at[source], back.at[source], cot_s, cot_r, k, seq(k)).wait_recv()
@@ -328,6 +323,12 @@
     for k in (1, 3, 2):
         copy_g(k).start()
     copy_relay(0).start()
+
+    def middle(n, _):
+        attend([4 * n + h for h in range(4)], (1, 2), qs, ks, vs, bias, attn)
+        return 0
+
+    lax.fori_loop(0, HEADS // 4, middle, 0)
     for copy in halo[:2]:
         copy.wait_recv()
     for tile in range(D // 128):
@@ -335,8 +336,8 @@
         xf[tile, :LEFT] = xb[:LEFT, cols].astype(F32)
         xf[tile, LEFT + F :] = xb[LEFT + F :, cols].astype(F32)
     conv_norm(
-        xf, taps, gain, dprev, dnext, hid, edge, 0, 6,
-        lambda n: (32 * n + 448 * (n // 4), 32 * n),
+        xf, taps, gain, dprev, dnext, hid, edge, 0, 3,
+        lambda n: (64 * n + 448 * (n // 2), 64 * n),
     )
     project(edge, slice(96, 160), wqkv, 0, qs, ((0, 32), (480, 32)))
     project(edge, slice(0, 192), wqkv, D, ks, ((0, 128), (576, 64)))
@@ -392,8 +393,6 @@
     def copy_audio(k):
         return remote(aout.at[(s + k) % N_SEQ], arecv.at[s], m_s, m_r, k, seq(k))
 
-    each(N_SEQ, lambda k: copy_audio(k).start())
-    arecv[s] = aout[s]
 
     for k in range(N_Y):
         copy_relay(k).wait_recv()
@@ -410,6 +409,8 @@
         return remote(block, got.at[k], xz_s, xz_r, k, across(k))
 
     each(N_X * N_GRP, lambda k: copy_xz(k).start())
+    each(N_SEQ, lambda k: copy_audio(k).start())
+    arecv[s] = aout[s]
     tile_sum = part[
         pl.ds(pl.multiple_of(x * 32, 32), 32), pl.ds(pl.multiple_of(z * 128, 128), 128)
     ]

time: 69.8 us -> 63.9 us (0.915)
  Pallas kernels: 67.1 us -> 61.2 us
    pallas_call x1, Pallas kernels: 67.1 us -> 61.2 us  [shards(): pl.pallas_call(whole_kernel, out_shape=(jax.ShapeDtypeStruct((128, D), BF...]
where the time goes in v5:
time: 63.9 us
  Pallas kernels  61.2 us (96%)
  local copies, waits for them, and re-layouts  2.02 us (3%)
  between operations  0.64 us (1%)
    pallas_call x1, Pallas kernels, shards(): pl.pallas_call(whole_kernel, out_shape=(jax.ShapeDtypeStruct((128, D), BF...  61.2 us
    unnamed x2, local copies, waits for them, and re-layouts  2.02 us

profile of v5, /device:TPU:1, one launch (start us, length us, event | category | flops | bytes accessed | tf_op | source)
XLA Modules:
  0.0 63.9 jit_solution(11894338232576216640)
XLA Ops:
  0.6 61.2 %whole.1 = (bf16[128,1024]{1,0:T(8,128)(2,1)S(1)}, bf16[4,2,4,32,1024]{4,3,2,1,0:T(8,128)(2,1)S(1)}) custom-call(bf16[1,512,1024]{2,1,0:T(8,128)(2,1)} %frames.1, s32[1,512]{1,0:T(1,128)} %begins.1, s32[1,64]{1,0:T(1,128)} %bitcast.7, f32[9,1024]{1,0:T(8,128)} %taps_hbm.1, f32[1,1024]{1,0:T(1,128)} %bitcast.6, bf16[1024,3072]{1,0:T(8,128)(2,1)} %wqkv_hbm.1, ...), custom_call_target="tpu_custom_call" | custom-call | tf_op jit(solution)/shard_map/whole/pallas_call | solution.py:519
  61.8 0.7 %copy.12 = bf16[1,128,1024]{2,1,0:T(8,128)(2,1)} copy(bf16[1,128,1024]{2,1,0:T(8,128)(2,1)S(1)} %bitcast.5) | data formatting | bytes 524288
  62.5 1.3 %copy.13 = bf16[1024,1024]{1,0:T(8,128)(2,1)} copy(bf16[1024,1024]{1,0:T(8,128)(2,1)S(1)} %bitcast.4) | data formatting | bytes 4194304

commit v6 on v5

--- a/solution.py
+++ b/solution.py
@@ -266,7 +266,7 @@
     loads[4].wait()
     to_slots(cotv[...], wide, cots)
     inner = lambda n: (128 + 64 * n, 64 * n)
-    conv_norm(xf, taps, gain, dprev, dnext, hid, nrm, 0, 4, inner)
+    conv_norm(xf, taps, gain, dprev, dnext, hid, nrm, 0, 2, inner)
     pl.semaphore_wait(barrier, N_SEQ - 1 + N_X * (N_GRP - 1))
 
     halo = [
@@ -288,7 +288,7 @@
         copy.start()
     back[s] = cots[s]
 
-    conv_norm(xf, taps, gain, dprev, dnext, hid, nrm, 4, 7, inner)
+    conv_norm(xf, taps, gain, dprev, dnext, hid, nrm, 2, 7, inner)
     loads[5].wait()
     place[...], pick[...] = placement_of(owner[...])
     loads[6].wait()
@@ -302,6 +302,12 @@
     bounds(marks, s * F, F * N_SEQ, dprev, dnext)
     attention_bias(dprev, dnext, bias)
 
+    def middle(n, _):
+        attend([4 * n + h for h in range(4)], (1, 2), qs, ks, vs, bias, attn)
+        return 0
+
+    lax.fori_loop(0, 1, middle, 0)
+
     def got_cot(k):
         source = (s + N_SEQ - k) % N_SEQ
         remote(back.at[source], back.at[source], cot_s, cot_r, k, seq(k)).wait_recv()
@@ -324,11 +330,7 @@
         copy_g(k).start()
     copy_relay(0).start()
 
-    def middle(n, _):
-        attend([4 * n + h for h in range(4)], (1, 2), qs, ks, vs, bias, attn)
-        return 0
-
-    lax.fori_loop(0, HEADS // 4, middle, 0)
+    lax.fori_loop(1, HEADS // 4, middle, 0)
     for copy in halo[:2]:
         copy.wait_recv()
     for tile in range(D // 128):
@@ -352,39 +354,41 @@
     ).astype(BF16)
 
     def copy_a(n):
-        return remote(asp.at[(j + n) % HEADS], aall.at[:, rows_of(j)], a_s, a_r, n, in_group(n))
-
-    def two_heads(n, m):
-        pair = ((j + n) % HEADS, (j + m) % HEADS)
+        return remote(asp.at[(j + n) % HEADS], aall.at[rows_of(j)], a_s, a_r, n, in_group(n))
+
+    def some_heads(*turns):
+        pair = [(j + n) % HEADS for n in turns]
         attend(pair, (0, 3), qs, ks, vs, bias, attn)
         for h in pair:
             lanes = pl.ds(pl.multiple_of(h * 128, 128), 128)
             asum = jnp.dot(gather, attn[:, lanes], preferred_element_type=F32)
             high = asum.astype(BF16)
             low = (asum - high.astype(F32)).astype(BF16)
-            ahl[0, :, lanes] = high
-            ahl[1, :, lanes] = low
-            asp[h, 0] = high
-            asp[h, 1] = low
+            ahl[:rows, lanes] = high
+            ahl[rows:, lanes] = low
+            asp[h, :, :128] = high
+            asp[h, :, 128:] = low
 
     def two_heads_and_send(p, _):
-        two_heads(2 * p + 1, 2 * p + 2)
+        some_heads(2 * p + 1, 2 * p + 2)
         copy_a(2 * p + 1).start()
         copy_a(2 * p + 2).start()
         return 0
 
-    lax.fori_loop(0, 3, two_heads_and_send, 0)
-    two_heads(7, 0)
-    copy_a(7).start()
-    aall[:, rows_of(j), :] = asp[j]
+    lax.fori_loop(0, 2, two_heads_and_send, 0)
+    some_heads(5, 6, 7)
+    for n in (5, 6, 7):
+        copy_a(n).start()
+    some_heads(0)
+    aall[rows_of(j), :] = asp[j]
     for k in (1, 3, 2):
         copy_g(k).wait_recv()
         copy_relay(k).start()
 
     loads[7].wait()
     hsum = jnp.dot(gather, hid[KOFF : KOFF + F, :], preferred_element_type=F32)
-    proj = jnp.dot(ahl[0], wout[...], preferred_element_type=F32)
-    proj = proj + jnp.dot(ahl[1], wout[...], preferred_element_type=F32)
+    proj = jnp.dot(ahl[...], wout[...], preferred_element_type=F32)
+    proj = proj[:rows] + proj[rows:]
     pooled = ((hsum + proj) * F32(1.0 / SUB)).astype(BF16)
     dims = (((0,), (0,)), ((), ()))
     outgoing = jnp.dot(place[...], pooled, preferred_element_type=F32)
@@ -398,8 +402,8 @@
         copy_relay(k).wait_recv()
 
     each(GROUP, lambda k: copy_a(k).wait_recv())
-    part[...] = lax.dot_general(aall[0], gall[...], dims, preferred_element_type=F32)
-    part[...] += lax.dot_general(aall[1], gall[...], dims, preferred_element_type=F32)
+    both = lax.dot_general(aall[...], gall[...], dims, preferred_element_type=F32)
+    part[...] = both[:128] + both[128:]
     for px in range(N_X):
         for pz in range(N_GRP):
             tiles[px, pz] = part[32 * px : 32 * px + 32, 128 * pz : 128 * pz + 128].astype(BF16)
@@ -408,7 +412,12 @@
         block = tiles.at[(x + k // N_GRP) % N_X, (z + k % N_GRP) % N_GRP]
         return remote(block, got.at[k], xz_s, xz_r, k, across(k))
 
-    each(N_X * N_GRP, lambda k: copy_xz(k).start())
+    far_first = (4, 3, 5, 2, 6, 1, 7)
+    for kz in far_first:
+        for kx in range(N_X):
+            copy_xz(kx * N_GRP + kz).start()
+    for kx in range(1, N_X):
+        copy_xz(kx * N_GRP).start()
     each(N_SEQ, lambda k: copy_audio(k).start())
     arecv[s] = aout[s]
     tile_sum = part[
@@ -424,7 +433,7 @@
         tile = fin.at[y, c, x, :, own_cols]
         return remote(tile, tile, t_s, t_r, k, grp(k))
 
-    for k in range(1, N_GRP):
+    for k in far_first:
         copy_t(k).start()
     for k in range(1, N_GRP):
         copy_t(k).wait_recv()
@@ -547,9 +556,9 @@
             pltpu.VMEM((1024, 128), F32),
             pltpu.VMEM((128, 64), BF16),
             pltpu.VMEM((64, 128), BF16),
-            pltpu.VMEM((2, 64, D), BF16),
-            pltpu.VMEM((HEADS, 2, 64, 128), BF16),
-            pltpu.VMEM((2, GROUP * 64, 128), BF16),
+            pltpu.VMEM((128, D), BF16),
+            pltpu.VMEM((HEADS, 64, 256), BF16),
+            pltpu.VMEM((GROUP * 64, 256), BF16),
             pltpu.VMEM((128, D), F32),
             pltpu.VMEM((N_X, N_GRP, 32, 128), BF16),
             pltpu.VMEM((N_X * N_GRP, 32, 128), BF16),

time: 63.9 us -> 62.9 us (0.984)
  Pallas kernels: 61.2 us -> 60.1 us
    pallas_call x1, Pallas kernels: 61.2 us -> 60.1 us  [shards(): pl.pallas_call(whole_kernel, out_shape=(jax.ShapeDtypeStruct((128, D), BF...]
where the time goes in v6:
time: 62.9 us; the launch traced here: 62.8 us
  Pallas kernels  60.1 us (96%)
  local copies, waits for them, and re-layouts  2.02 us (3%)
  between operations  0.64 us (1%)
    pallas_call x1, Pallas kernels, shards(): pl.pallas_call(whole_kernel, out_shape=(jax.ShapeDtypeStruct((128, D), BF...  60.1 us
    unnamed x2, local copies, waits for them, and re-layouts  2.02 us

profile of v6, /device:TPU:1, one launch (start us, length us, event | category | flops | bytes accessed | tf_op | source)
XLA Modules:
  0.0 62.8 jit_solution(14255291880804403328)
XLA Ops:
  0.6 60.1 %whole.1 = (bf16[128,1024]{1,0:T(8,128)(2,1)S(1)}, bf16[4,2,4,32,1024]{4,3,2,1,0:T(8,128)(2,1)S(1)}) custom-call(bf16[1,512,1024]{2,1,0:T(8,128)(2,1)} %frames.1, s32[1,512]{1,0:T(1,128)} %begins.1, s32[1,64]{1,0:T(1,128)} %bitcast.7, f32[9,1024]{1,0:T(8,128)} %taps_hbm.1, f32[1,1024]{1,0:T(1,128)} %bitcast.6, bf16[1024,3072]{1,0:T(8,128)(2,1)} %wqkv_hbm.1, ...), custom_call_target="tpu_custom_call" | custom-call | tf_op jit(solution)/shard_map/whole/pallas_call | solution.py:528
  60.8 0.7 %copy.12 = bf16[1,128,1024]{2,1,0:T(8,128)(2,1)} copy(bf16[1,128,1024]{2,1,0:T(8,128)(2,1)S(1)} %bitcast.5) | data formatting | bytes 524288
  61.5 1.3 %copy.13 = bf16[1024,1024]{1,0:T(8,128)(2,1)} copy(bf16[1024,1024]{1,0:T(8,128)(2,1)S(1)} %bitcast.4) | data formatting | bytes 4194304

commit v7 on v6

--- a/solution.py
+++ b/solution.py
@@ -369,13 +369,9 @@
             asp[h, :, :128] = high
             asp[h, :, 128:] = low
 
-    def two_heads_and_send(p, _):
-        some_heads(2 * p + 1, 2 * p + 2)
-        copy_a(2 * p + 1).start()
-        copy_a(2 * p + 2).start()
-        return 0
-
-    lax.fori_loop(0, 2, two_heads_and_send, 0)
+    some_heads(1, 2, 3, 4)
+    for n in (1, 2, 3, 4):
+        copy_a(n).start()
     some_heads(5, 6, 7)
     for n in (5, 6, 7):
         copy_a(n).start()
@@ -385,19 +381,7 @@
         copy_g(k).wait_recv()
         copy_relay(k).start()
 
-    loads[7].wait()
-    hsum = jnp.dot(gather, hid[KOFF : KOFF + F, :], preferred_element_type=F32)
-    proj = jnp.dot(ahl[...], wout[...], preferred_element_type=F32)
-    proj = proj[:rows] + proj[rows:]
-    pooled = ((hsum + proj) * F32(1.0 / SUB)).astype(BF16)
     dims = (((0,), (0,)), ((), ()))
-    outgoing = jnp.dot(place[...], pooled, preferred_element_type=F32)
-    to_slots(outgoing, wide, aout)
-
-    def copy_audio(k):
-        return remote(aout.at[(s + k) % N_SEQ], arecv.at[s], m_s, m_r, k, seq(k))
-
-
     for k in range(N_Y):
         copy_relay(k).wait_recv()
 
@@ -418,6 +402,17 @@
             copy_xz(kx * N_GRP + kz).start()
     for kx in range(1, N_X):
         copy_xz(kx * N_GRP).start()
+    loads[7].wait()
+    hsum = jnp.dot(gather, hid[KOFF : KOFF + F, :], preferred_element_type=F32)
+    proj = jnp.dot(ahl[...], wout[...], preferred_element_type=F32)
+    proj = proj[:rows] + proj[rows:]
+    pooled = ((hsum + proj) * F32(1.0 / SUB)).astype(BF16)
+    outgoing = jnp.dot(place[...], pooled, preferred_element_type=F32)
+    to_slots(outgoing, wide, aout)
+
+    def copy_audio(k):
+        return remote(aout.at[(s + k) % N_SEQ], arecv.at[s], m_s, m_r, k, seq(k))
+
     each(N_SEQ, lambda k: copy_audio(k).start())
     arecv[s] = aout[s]
     tile_sum = part[
@@ -456,13 +451,10 @@
         block = fin.at[(y + N_Y - ky) % N_Y, c, x, :, second]
         return remote(block, block, p1_s, p1_r, ky * N_X + kx, along_x(kx))
 
-    def copy_c0(k):
-        block = fin.at[(y + N_Y - k) % N_Y, c, :, :, first]
-        return remote(block, block, c_s, c_r, k, other_core)
-
-    def copy_c1(k):
-        block = fin.at[:, c, (x + N_X - k) % N_X, :, second]
-        return remote(block, block, c_s, c_r, N_Y + k, other_core)
+    def copy_c(half, ky, kx):
+        cols = (first, second)[half]
+        block = fin.at[(y + N_Y - ky) % N_Y, c, (x + N_X - kx) % N_X, :, cols]
+        return remote(block, block, c_s, c_r, (half * N_Y + ky) * N_X + kx, other_core)
 
     for k in (1, 3, 2):
         copy_h0(k).start()
@@ -470,15 +462,17 @@
     for k in (1, 3, 2):
         copy_p0(0, k).start()
         copy_p1(0, k).start()
+    copy_c(0, 0, 0).start()
+    copy_c(1, 0, 0).start()
     for k in (1, 3, 2):
         copy_h0(k).wait_recv()
         for ky in (1, 3, 2):
             copy_p0(k, ky).start()
+        copy_c(0, 0, k).start()
         copy_h1(k).wait_recv()
         for kx in (1, 3, 2):
             copy_p1(k, kx).start()
-    copy_c0(0).start()
-    copy_c1(0).start()
+        copy_c(1, k, 0).start()
 
     def got_audio(k):
         source = (s + N_SEQ - k) % N_SEQ
@@ -488,17 +482,16 @@
     for tile, value in enumerate(from_slots(arecv, wide)):
         audio[:, 128 * tile : 128 * tile + 128] = value
 
-    for k in (1, 3, 2):
-        for other in range(N_X):
+    for other in (0, 1, 3, 2):
+        for k in (1, 3, 2):
             copy_p0(other, k).wait_recv()
-        copy_c0(k).start()
-        for other in range(N_Y):
+            copy_c(0, k, other).start()
             copy_p1(other, k).wait_recv()
-        copy_c1(k).start()
-    for k in range(N_Y):
-        copy_c0(k).wait_recv()
-        copy_c1(k).wait_recv()
-
+            copy_c(1, other, k).start()
+    for ky in range(N_Y):
+        for kx in range(N_X):
+            copy_c(0, ky, kx).wait_recv()
+            copy_c(1, ky, kx).wait_recv()
     for copy in halo:
         copy.wait_send()
 
@@ -514,8 +507,9 @@
         copy_h1(k).wait_send()
     for k in range(N_Y):
         copy_relay(k).wait_send()
-        copy_c0(k).wait_send()
-        copy_c1(k).wait_send()
+        for kx in range(N_X):
+            copy_c(0, k, kx).wait_send()
+            copy_c(1, k, kx).wait_send()
         for other in range(1, N_X):
             copy_p0(k, other).wait_send()
             copy_p1(k, other).wait_send()
@@ -580,7 +574,7 @@
             dma((N_Y,)), dma((N_Y,)),
             dma((N_X * N_Y,)), dma((N_X * N_Y,)),
             dma((N_X * N_Y,)), dma((N_X * N_Y,)),
-            dma((2 * N_Y,)), dma((2 * N_Y,)),
+            dma((2 * N_Y * N_X,)), dma((2 * N_Y * N_X,)),
         ],
         compiler_params=pltpu.CompilerParams(
             vmem_limit_bytes=48 * 1024 * 1024, collective_id=0, has_side_effects=True

time: 62.9 us -> 63 us (level)
  no operation moved by 1% of the time
where the time goes in v7:
time: 63 us; the launch traced here: 62.9 us
  Pallas kernels  60.2 us (96%)
  local copies, waits for them, and re-layouts  2.02 us (3%)
  between operations  0.64 us (1%)
    pallas_call x1, Pallas kernels, shards(): pl.pallas_call(whole_kernel, out_shape=(jax.ShapeDtypeStruct((128, D), BF...  60.2 us
    unnamed x2, local copies, waits for them, and re-layouts  2.02 us

profile of v7, /device:TPU:1, one launch (start us, length us, event | category | flops | bytes accessed | tf_op | source)
XLA Modules:
  0.0 62.9 jit_solution(16118908126854461853)
XLA Ops:
  0.6 60.2 %whole.1 = (bf16[128,1024]{1,0:T(8,128)(2,1)S(1)}, bf16[4,2,4,32,1024]{4,3,2,1,0:T(8,128)(2,1)S(1)}) custom-call(bf16[1,512,1024]{2,1,0:T(8,128)(2,1)} %frames.1, s32[1,512]{1,0:T(1,128)} %begins.1, s32[1,64]{1,0:T(1,128)} %bitcast.7, f32[9,1024]{1,0:T(8,128)} %taps_hbm.1, f32[1,1024]{1,0:T(1,128)} %bitcast.6, bf16[1024,3072]{1,0:T(8,128)(2,1)} %wqkv_hbm.1, ...), custom_call_target="tpu_custom_call" | custom-call | tf_op jit(solution)/shard_map/whole/pallas_call | solution.py:522
  60.9 0.7 %copy.12 = bf16[1,128,1024]{2,1,0:T(8,128)(2,1)} copy(bf16[1,128,1024]{2,1,0:T(8,128)(2,1)S(1)} %bitcast.5) | data formatting | bytes 524288
  61.6 1.3 %copy.13 = bf16[1024,1024]{1,0:T(8,128)(2,1)} copy(bf16[1024,1024]{1,0:T(8,128)(2,1)S(1)} %bitcast.4) | data formatting | bytes 4194304
